TPU v7x, 128 devices: a whole 4x4x4 slice. The times are simulated.
128 devices in a mesh: comp: 2 (over y_hi), gy: 4 (over y_lo, core), gx: 16 (over z, x).
Axes of the slice: x: 4, y: 4 (y_hi: 2, y_lo: 2; y = y_hi * 2 + y_lo), z: 4, core: 2. Of those that a mesh axis runs over, the one named last changes fastest.
Arguments:
- state: float32 [2, 8, 512, 2048], P('comp', None, 'gy', 'gx'), may hold values from -6 to 6
- target: float32 [2, 8, 512, 2048], P('comp', None, 'gy', 'gx'), may hold values from -2.5 to 0.5
- land_mask: int32 [2, 512, 2048], P('comp', 'gy', 'gx'), may hold values 0 or 1
- diffusivity: float32 [2, 8], replicated, may hold values from 0.03 to 0.24
- coupling: float32 [2, 8, 4], replicated, may hold values from -3 to 3
- w_in: bfloat16 [16, 256], replicated, may hold values from -1.5 to 1.5
- b_in: float32 [256], replicated, may hold values from -3 to 3
- w_mid: bfloat16 [256, 256], replicated, may hold values from -0.375 to 0.375
- b_mid: float32 [256], replicated, may hold values from -3 to 3
- w_out: bfloat16 [256, 4], replicated, may hold values from -0.375 to 0.375
- b_out: float32 [4], replicated, may hold values from -3 to 3
- remap_weight: bfloat16 [2, 4, 16, 64, 4, 128, 128], P('comp', 'gy', 'gx'), may hold values from -0.5 to 0.5
- remap_source: int32 [2, 4, 16, 64, 4], P('comp', 'gy', 'gx'), may hold values from 0 to 127
- remap_target: int32 [2, 4, 16, 64, 4], P('comp', 'gy', 'gx'), may hold values from 0 to 127
- remap_count: int32 [2, 4, 16, 64], P('comp', 'gy', 'gx'), may hold values from 0 to 4, as said below
Outputs:
- new_state: float32 [2, 8, 512, 2048], P('comp', None, 'gy', 'gx')
- state_adjoint: float32 [2, 8, 512, 2048], P('comp', None, 'gy', 'gx')
- grad_w_in: float32 [16, 256], replicated
- grad_b_in: float32 [256], replicated
- grad_w_mid: float32 [256, 256], replicated
- grad_b_mid: float32 [256], replicated
- grad_w_out: float32 [256, 4], replicated
- grad_b_out: float32 [4], replicated
Inputs may be any that keep to these rules, and one draw needn't show every extreme that they name: remap_count[c, i, j, q] leading slots of the pair are in use, the rest are padding. A pair has slots in use exactly where receiving tile q lies within 2 tile rows of i and in a tile column within 2 of j (periodic), or, for a sender in the top tile row, where q lies in the top tile row within 1 column (periodic) of column 15 - j; such pairs use 1 slot or more; for each component one receiving tile has all 4 slots in use from every such sending tile.
All inputs are finite; a program needn't handle non-finite values. No bound on the sum of `land_mask` on one device may be relied on, other than what follows from the above.
Results may differ from a plain program's by a relative error of at most 0.0037.
Values may be sent and summed in bfloat16 or wider, within the bound.
A program may use at most 64 MiB of HBM per device.

v0:
```python
import math

import jax
import jax.numpy as jnp
from jax import lax
from jax.sharding import PartitionSpec as P

PRECISE = lax.Precision.HIGHEST


def extended(cells, sides, width, closed):
    for axis, dim in sides:
        count = lax.axis_size(axis)
        ends = count if closed else count - 1
        head = lax.slice_in_dim(cells, 0, width, axis=dim)
        tail = lax.slice_in_dim(cells, cells.shape[dim] - width, cells.shape[dim], axis=dim)
        cells = jnp.concatenate(
            [
                lax.ppermute(tail, axis, [(i, (i + 1) % count) for i in range(ends)]),
                cells,
                lax.ppermute(head, axis, [((i + 1) % count, i) for i in range(ends)]),
            ],
            axis=dim,
        )
    return cells


def partner(block, axis, stride):
    count = lax.axis_size(axis)
    route = []
    for low in range(count):
        high = low | 1 << stride
        if high != low and high < count:
            route += [(low, high), (high, low)]
    return lax.ppermute(block, axis, route)


def silu_slope(preact):
    sigmoid_value = jax.nn.sigmoid(preact)
    return sigmoid_value * (1.0 + preact * (1.0 - sigmoid_value))


def laplace(surface, on_fold):
    wide_field = extended(surface, (("gx", 2),), 1, True)
    tall_field = extended(surface, (("gy", 1),), 1, False)
    top_row = surface[:, -1, :]
    tile_width = top_row.shape[1]
    whole_row = lax.all_gather(top_row, "gx", axis=1, tiled=True)
    mirrored = lax.dynamic_slice_in_dim(
        whole_row[:, ::-1], lax.axis_index("gx") * tile_width, tile_width, 1
    )
    north_rows = tall_field[:, 2:, :]
    north_rows = north_rows.at[:, -1, :].add(jnp.where(on_fold, mirrored, 0.0))
    return (
        wide_field[:, :, 2:]
        + wide_field[:, :, :-2]
        + tall_field[:, :-2, :]
        + north_rows
        - 4.0 * surface
    )


def forward_route(outgoing):
    relayed = lax.all_to_all(outgoing, ("gy", "gx"), split_axis=0, concat_axis=0, tiled=True)
    arrived = partner(relayed, "comp", 0)
    return arrived


def return_route(outgoing):
    relayed = lax.all_to_all(outgoing, ("gy", "gx"), split_axis=0, concat_axis=0, tiled=True)
    arrived = partner(relayed, "comp", 0)
    return arrived


def shards(
    state,
    target,
    land_mask,
    diffusivity,
    coupling,
    w_in,
    b_in,
    w_mid,
    b_mid,
    w_out,
    b_out,
    remap_weight,
    remap_source,
    remap_target,
    remap_count,
):
    comp_index = lax.axis_index("comp")
    is_ocean = comp_index == 1
    on_fold = jnp.logical_and(is_ocean, lax.axis_index("gy") == lax.axis_size("gy") - 1)
    surface = state[0]
    channels, tile_rows, tile_width = surface.shape
    cell_count = tile_rows * tile_width
    peer_count = remap_source.shape[3]
    slot_count = remap_source.shape[4]
    pair_count = peer_count * slot_count
    wet_mask = land_mask[0].astype(jnp.float32).reshape(1, cell_count)
    diff_mask = jnp.where(is_ocean, wet_mask, 1.0)
    diffuse_rate = diffusivity[comp_index]
    couple = coupling[comp_index]
    rounded = surface.astype(jnp.bfloat16)
    source = remap_source[0, 0, 0].reshape(pair_count)
    kernels = remap_weight[0, 0, 0].reshape(pair_count, tile_width, tile_width)
    slot_index = lax.broadcasted_iota(jnp.int32, (peer_count, slot_count), 1)
    live_mask = (
        (slot_index < remap_count[0, 0, 0][:, None]).astype(jnp.float32).reshape(pair_count, 1, 1)
    )
    picked = rounded[:, source, :]
    outgoing = (
        jnp.einsum("cki,kij->kcj", picked, kernels, preferred_element_type=jnp.float32) * live_mask
    )
    arrived = forward_route(outgoing.reshape(peer_count, slot_count, channels, tile_width))
    laplacian = laplace(surface, on_fold).reshape(channels, cell_count)
    row_index = lax.broadcasted_iota(jnp.int32, (tile_rows, pair_count), 0)
    landing = (row_index == remap_target[0, 0, 0].reshape(1, pair_count)).astype(jnp.float32)
    remapped = jnp.einsum(
        "tk,kcj->ctj", landing, arrived.reshape(pair_count, channels, tile_width), precision=PRECISE
    )
    own_fields = rounded.reshape(channels, cell_count)
    other_fields = remapped.astype(jnp.bfloat16).reshape(channels, cell_count)
    features = jnp.concatenate(
        [
            jnp.where(is_ocean, other_fields, own_fields),
            jnp.where(is_ocean, own_fields, other_fields),
        ],
        axis=0,
    )
    current = surface.reshape(channels, cell_count)
    goal = target[0].reshape(channels, cell_count)
    block_size = math.gcd(cell_count, 2048)

    def advance(block_index, loop_state):
        new_fields, misfits, feature_cots, gradients = loop_state
        offset = block_index * block_size

        def take_block(array):
            return lax.dynamic_slice_in_dim(array, offset, block_size, 1)

        feature_block = take_block(features)
        wet_block = take_block(wet_mask)
        diff_block = take_block(diff_mask)
        pre_first = (
            jnp.einsum("fh,fn->hn", w_in, feature_block, preferred_element_type=jnp.float32)
            + b_in[:, None]
        )
        hidden_first = jax.nn.silu(pre_first).astype(jnp.bfloat16)
        pre_second = (
            jnp.einsum("hk,hn->kn", w_mid, hidden_first, preferred_element_type=jnp.float32)
            + b_mid[:, None]
        )
        hidden_second = jax.nn.silu(pre_second).astype(jnp.bfloat16)
        fluxes = (
            jnp.einsum("ho,hn->on", w_out, hidden_second, preferred_element_type=jnp.float32)
            + b_out[:, None]
        ) * wet_block
        updated = (
            take_block(current)
            + diffuse_rate[:, None] * diff_block * take_block(laplacian)
            + jnp.dot(couple, fluxes, precision=PRECISE)
        )
        misfit = updated - take_block(goal)
        flux_cot = (wet_block * jnp.dot(couple.T, misfit, precision=PRECISE)).astype(jnp.bfloat16)
        second_cot = (
            jnp.einsum("ho,on->hn", w_out, flux_cot, preferred_element_type=jnp.float32)
            * silu_slope(pre_second)
        ).astype(jnp.bfloat16)
        first_cot = (
            jnp.einsum("hk,kn->hn", w_mid, second_cot, preferred_element_type=jnp.float32)
            * silu_slope(pre_first)
        ).astype(jnp.bfloat16)
        feature_cot = jnp.einsum("fh,hn->fn", w_in, first_cot, preferred_element_type=jnp.float32)
        additions = (
            jnp.einsum("fn,hn->fh", feature_block, first_cot, preferred_element_type=jnp.float32),
            jnp.sum(first_cot.astype(jnp.float32), axis=1),
            jnp.einsum("hn,kn->hk", hidden_first, second_cot, preferred_element_type=jnp.float32),
            jnp.sum(second_cot.astype(jnp.float32), axis=1),
            jnp.einsum("hn,on->ho", hidden_second, flux_cot, preferred_element_type=jnp.float32),
            jnp.sum(flux_cot.astype(jnp.float32), axis=1),
        )
        new_fields = lax.dynamic_update_slice_in_dim(new_fields, updated, offset, 1)
        misfits = lax.dynamic_update_slice_in_dim(misfits, misfit, offset, 1)
        feature_cots = lax.dynamic_update_slice_in_dim(feature_cots, feature_cot, offset, 1)
        return (new_fields, misfits, feature_cots, jax.tree.map(jnp.add, gradients, additions))

    initial = (
        jnp.zeros((channels, cell_count), jnp.float32),
        jnp.zeros((channels, cell_count), jnp.float32),
        jnp.zeros((2 * channels, cell_count), jnp.float32),
        (
            jnp.zeros(w_in.shape, jnp.float32),
            jnp.zeros(b_in.shape, jnp.float32),
            jnp.zeros(w_mid.shape, jnp.float32),
            jnp.zeros(b_mid.shape, jnp.float32),
            jnp.zeros(w_out.shape, jnp.float32),
            jnp.zeros(b_out.shape, jnp.float32),
        ),
    )
    new_fields, misfits, feature_cots, gradients = lax.fori_loop(
        0, cell_count // block_size, advance, initial
    )
    back_lap = laplace((diff_mask * misfits).reshape(channels, tile_rows, tile_width), on_fold)
    own_cot = jnp.where(is_ocean, feature_cots[channels:], feature_cots[:channels]).reshape(
        channels, tile_rows, tile_width
    )
    other_cot = jnp.where(is_ocean, feature_cots[:channels], feature_cots[channels:]).reshape(
        channels, tile_rows, tile_width
    )
    going_back = jnp.einsum("tk,ctj->kcj", landing, other_cot, precision=PRECISE).astype(
        jnp.bfloat16
    )
    returned = return_route(going_back.reshape(peer_count, slot_count, channels, tile_width))
    spread = (
        jnp.einsum(
            "kcj,kij->kci",
            returned.reshape(pair_count, channels, tile_width),
            kernels,
            preferred_element_type=jnp.float32,
        )
        * live_mask
    )
    anchor = (row_index == source.reshape(1, pair_count)).astype(jnp.float32)
    remap_back = jnp.einsum("tk,kci->cti", anchor, spread, precision=PRECISE)
    adjoint_field = (
        misfits.reshape(channels, tile_rows, tile_width)
        + diffuse_rate[:, None, None] * back_lap
        + own_cot
        + remap_back
    )
    grad_first, bias_first, grad_second, bias_second, grad_third, bias_third = gradients
    grad_first, bias_first, grad_second, bias_second, grad_third, bias_third = lax.psum(
        (grad_first, bias_first, grad_second, bias_second, grad_third, bias_third),
        ("comp", "gy", "gx"),
    )
    scale = 1.0 / (cell_count * lax.axis_size("gy") * lax.axis_size("gx"))
    return (
        new_fields.reshape(1, channels, tile_rows, tile_width),
        adjoint_field.reshape(1, channels, tile_rows, tile_width),
        grad_first * scale,
        bias_first * scale,
        grad_second * scale,
        bias_second * scale,
        grad_third * scale,
        bias_third * scale,
    )


def solution(mesh):
    placed = (
        P("comp", None, "gy", "gx"),
        P("comp", None, "gy", "gx"),
        P("comp", "gy", "gx"),
        P(),
        P(),
        P(),
        P(),
        P(),
        P(),
        P(),
        P(),
        P("comp", "gy", "gx", None, None, None, None),
        P("comp", "gy", "gx", None, None),
        P("comp", "gy", "gx", None, None),
        P("comp", "gy", "gx", None),
    )
    return jax.shard_map(
        shards,
        mesh=mesh,
        in_specs=placed,
        out_specs=(
            P("comp", None, "gy", "gx"),
            P("comp", None, "gy", "gx"),
            P(),
            P(),
            P(),
            P(),
            P(),
            P(),
        ),
        check_vma=False,
    )
```

profile of v0, /device:TPU:0, one launch (start us, length us, event | category | flops | bytes accessed | tf_op | source)
XLA Modules:
  0.0 558.9 jit_solution(4015643572579584607)
XLA Ops:
  10.0 3.9 collective-permute-start.2
  13.8 6.4 %collective-permute-start = (f32[8,128,1]{1,2,0:T(1,128)S(1)}, f32[8,128,1]{1,2,0:T(1,128)S(1)}, u32[]{:S(2)}, u32[]{:S(2)}) collective-permute-start(f32[8,128,1]{1,2,0:T(1,128)S(1)} %get-tuple-element.625), channel_id=1, source_target_pairs={{1,0},{2,1},{3,2},{4,3},{5,4},{6,5},{7,6},{8,7},{9,8},{10,9},{11,1... | collective-permute-start | bytes 12296 | tf_op jit(solution)/shard_map/ppermute | solution.py:21
  21.7 6.7 %convolution_multiply_fusion.2 = f32[256,8,128]{2,1,0:T(8,128)} fusion(bf16[256,128,128]{2,1,0:T(8,128)(2,1)} %bitcast.179, bf16[256,8,128]{2,1,0:T(8,128)(2,1)S(1)} %gather_fusion, f32[256]{0:T(256)S(1)} %reshape.210), kind=kOutput, calls=%fused_computation.44 | convolution fusion | flops 67371008 | bytes 9962496 | tf_op jit(solution)/shard_map/cki,kij->kcj/dot_general | solution.py:114
  28.4 8.1 %all-to-all-start = ((f32[64,4,8,128]{3,2,1,0:T(8,128)}), f32[64,4,8,128]{3,2,1,0:T(8,128)}, u32[]{:S(2)}, u32[]{:S(2)}) async-start(f32[64,4,8,128]{3,2,1,0:T(8,128)} %bitcast.7), calls=%async_computation | async-start | bytes 2097152 | tf_op jit(solution)/shard_map/all_to_all | solution.py:64
  36.5 61.9 %all-gather = f32[8,1,2048]{1,2,0:T(8,128)} all-gather(f32[8,1,128]{1,2,0:T(8,128)S(1)} %get-tuple-element.627), channel_id=2, replica_groups=mesh['comp'=2,'gy'=4,'gx'=16] {'gx'}, dimensions={2}, use_global_device_ids=true | all-gather | bytes 69632 | tf_op jit(solution)/shard_map/all_gather | solution.py:48
  98.4 5.7 %reduce.5 = f32[8,2048]{1,0:T(8,128)S(1)} reduce(f32[8,1,2048]{1,2,0:T(8,128)} %all-gather, f32[]{:T(128)} %constant.146), dimensions={1}, to_apply=%all-gather.reduce_sub_computation | reduce | bytes 131076 | tf_op jit(solution)/shard_map/all_gather | solution.py:48
  108.4 2.7 scatter-add.6
  112.8 3.2 collective-permute-start.4
  117.6 20.1 %collective-permute-done.4 = f32[64,4,8,128]{3,2,1,0:T(8,128)S(1)} collective-permute-done((f32[64,4,8,128]{3,2,1,0:T(8,128)}, f32[64,4,8,128]{3,2,1,0:T(8,128)S(1)}, u32[]{:S(2)}, u32[]{:S(2)}) %collective-permute-start.4) | collective-permute-done | bytes 1048608 | tf_op jit(solution)/shard_map/ppermute | solution.py:35
  142.3 103.9 %while.32 = (s32[]{:T(128)}, f32[8,16384]{1,0:T(8,128)}, f32[8,16384]{1,0:T(8,128)}, f32[16,16384]{1,0:T(8,128)}, f32[16,256]{1,0:T(8,128)S(1)}, /*index=5*/f32[...) while((s32[]{:T(128)}, f32[8,16384]{1,0:T(8,128)}, ...), condition=%wide.region_4.5_spmd.clone, body=%wide.region_0.4_spmd.clone.sunk | while | flops 890530304 | bytes 31177564 | solution.py:202
  149.4 2.6 convert_reduce_fusion.7
  162.4 2.6 convert_reduce_fusion.7
  175.4 2.6 convert_reduce_fusion.7
  201.4 2.6 convert_reduce_fusion.7
  227.4 2.6 convert_reduce_fusion.7
  240.4 2.6 convert_reduce_fusion.7
  246.3 64.0 %all-reduce = (f32[16,256]{1,0:T(8,128)S(1)}, f32[256]{0:T(256)S(1)}, f32[256]{0:T(256)S(1)}, f32[256,4]{0,1:T(4,128)S(1)}, f32[4]{0:T(128)S(1)}) all-reduce(f32[16,256]{1,0:T(8,128)S(1)} %get-tuple-element.422, f32[256]{0:T(256)S(1)} %get-tuple-element.423, ...), channel_id=1, replica_groups=mesh['comp'=2,'gy'=4,'gx'=16] {'comp','gy','gx'}, use_global_device_ids=true, to_apply=%region_5.6 | all-reduce | flops 5636 | bytes 45088 | tf_op jit(solution)/shard_map/psum | solution.py:234
  314.9 5.8 %all-to-all-start.1 = ((bf16[64,4,8,128]{3,1,2,0:T(4,128)(2,1)}), bf16[64,4,8,128]{3,1,2,0:T(4,128)(2,1)}, u32[]{:S(2)}, u32[]{:S(2)}) async-start(bf16[64,4,8,128]{3,1,2,0:T(4,128)(2,1)} %copy.144), calls=%async_computation.1 | async-start | bytes 1048576 | tf_op jit(solution)/shard_map/all_to_all | solution.py:70
  322.9 10.3 %all-to-all-done.1 = bf16[64,4,8,128]{3,1,2,0:T(4,128)(2,1)} async-done(((bf16[64,4,8,128]{3,1,2,0:T(4,128)(2,1)}), bf16[64,4,8,128]{3,1,2,0:T(4,128)(2,1)}, u32[]{:S(2)}, u32[]{:S(2)}) %all-to-all-start.1) | async-done | bytes 524320 | tf_op jit(solution)/shard_map/all_to_all | solution.py:70
  337.5 50.8 %all-gather.1 = f32[8,1,2048]{1,2,0:T(8,128)} all-gather(f32[8,1,128]{1,2,0:T(8,128)} %get-tuple-element.623), channel_id=3, replica_groups=mesh['comp'=2,'gy'=4,'gx'=16] {'gx'}, dimensions={2}, use_global_device_ids=true | all-gather | bytes 69632 | tf_op jit(solution)/shard_map/all_gather | solution.py:48
  388.3 5.6 %reduce.6 = f32[8,2048]{1,0:T(8,128)S(1)} reduce(f32[8,1,2048]{1,2,0:T(8,128)} %all-gather.1, f32[]{:T(128)} %constant.146), dimensions={1}, to_apply=%all-gather.1.reduce_sub_computation | reduce | bytes 131076 | tf_op jit(solution)/shard_map/all_gather | solution.py:48
  396.9 2.7 collective-permute-start.5
  407.2 131.9 %all-reduce.3.cloned.1.call-done = f32[256,256]{1,0:T(8,128)} async-done(((f32[256,256]{1,0:T(8,128)}), f32[256,256]{1,0:T(8,128)}) %all-reduce.3.cloned.1.call-update) | async-done | bytes 262160 | tf_op jit(solution)/shard_map/psum | solution.py:234
  541.9 6.7 %convolution_multiply_fusion.1 = f32[256,8,128]{2,1,0:T(8,128)S(1)} fusion(bf16[256,8,128]{2,1,0:T(8,128)(2,1)S(1)} %bitcast.186, bf16[256,128,128]{2,1,0:T(8,128)(2,1)} %bitcast.180, f32[256]{0:T(256)S(1)} %reshape.210), kind=kOutput, calls=%fused_computation.43 | convolution fusion | flops 67371008 | bytes 9962496 | tf_op jit(solution)/shard_map/kcj,kij->kci/dot_general | solution.py:217
  (327 shorter events, 131.2 us)
Async XLA Ops:
  7.2 98.2 %copy-start = (f32[2,8,4]{1,2,0:T(4,128)S(1)}, f32[2,8,4]{1,2,0:T(4,128)}, u32[]{:S(2)}) copy-start(f32[2,8,4]{1,2,0:T(4,128)} %param.25) | copy-start | bytes 772
  7.2 13.3 %copy-start.13 = (s32[1,1,1,64,4]{3,4,2,1,0:T(4,128)S(1)}, s32[1,1,1,64,4]{3,4,2,1,0:T(4,128)}, u32[]{:S(2)}) copy-start(s32[1,1,1,64,4]{3,4,2,1,0:T(4,128)} %param.33) | copy-start | bytes 3076
  7.2 13.5 %copy-start.15 = (s32[1,1,1,64]{3,2,1,0:T(1,128)S(1)}, s32[1,1,1,64]{3,2,1,0:T(1,128)}, u32[]{:S(2)}) copy-start(s32[1,1,1,64]{3,2,1,0:T(1,128)} %param.35) | copy-start | bytes 772
  8.7 98.5 %collective-permute-start.3 = (f32[8,1,128]{1,2,0:T(8,128)S(1)}, f32[8,1,128]{1,2,0:T(8,128)S(1)}, u32[]{:S(2)}, u32[]{:S(2)}) collective-permute-start(f32[8,1,128]{1,2,0:T(8,128)S(1)} %get-tuple-element.628), channel_id=1, source_target_pairs={{16,0},{32,16},{48,32},{17,1},{33,17},{49,33},{18,2},{34,18},{50,3... | collective-permute-start | bytes 12296 | tf_op jit(solution)/shard_map/ppermute | solution.py:21
  10.0 101.1 %collective-permute-start.2 = (f32[8,1,128]{1,2,0:T(8,128)S(1)}, f32[8,1,128]{1,2,0:T(8,128)}, u32[]{:S(2)}, u32[]{:S(2)}) collective-permute-start(f32[8,1,128]{1,2,0:T(8,128)S(1)} %get-tuple-element.627), channel_id=1, source_target_pairs={{0,16},{16,32},{32,48},{1,17},{17,33},{33,49},{2,18},{18,34},{34,5... | collective-permute-start | bytes 12296 | tf_op jit(solution)/shard_map/ppermute | solution.py:19
  13.8 97.2 %collective-permute-start = (f32[8,128,1]{1,2,0:T(1,128)S(1)}, f32[8,128,1]{1,2,0:T(1,128)S(1)}, u32[]{:S(2)}, u32[]{:S(2)}) collective-permute-start(f32[8,128,1]{1,2,0:T(1,128)S(1)} %get-tuple-element.625), channel_id=1, source_target_pairs={{1,0},{2,1},{3,2},{4,3},{5,4},{6,5},{7,6},{8,7},{9,8},{10,9},{11,1... | collective-permute-start | bytes 12296 | tf_op jit(solution)/shard_map/ppermute | solution.py:21
  20.2 90.9 %collective-permute-start.1 = (f32[8,128,1]{1,2,0:T(1,128)S(1)}, f32[8,128,1]{1,2,0:T(1,128)S(1)}, u32[]{:S(2)}, u32[]{:S(2)}) collective-permute-start(f32[8,128,1]{1,2,0:T(1,128)S(1)} %get-tuple-element.626), channel_id=1, source_target_pairs={{0,1},{1,2},{2,3},{3,4},{4,5},{5,6},{6,7},{7,8},{8,9},{9,10},{10,1... | collective-permute-start | bytes 12296 | tf_op jit(solution)/shard_map/ppermute | solution.py:19
  28.4 84.4 %all-to-all-start = ((f32[64,4,8,128]{3,2,1,0:T(8,128)}), f32[64,4,8,128]{3,2,1,0:T(8,128)}, u32[]{:S(2)}, u32[]{:S(2)}) async-start(f32[64,4,8,128]{3,2,1,0:T(8,128)} %bitcast.7), calls=%async_computation | async-start | bytes 2097152 | tf_op jit(solution)/shard_map/all_to_all | solution.py:64
  98.4 6.9 %copy-start.9 = (s32[1,128,128]{2,1,0:T(8,128)S(1)}, s32[1,128,128]{2,1,0:T(8,128)}, u32[]{:S(2)}) copy-start(s32[1,128,128]{2,1,0:T(8,128)} %param.23) | copy-start | bytes 196612
  98.4 7.0 %copy-start.18 = (f32[2,8]{1,0:T(2,128)S(1)}, f32[2,8]{1,0:T(2,128)}, u32[]{:S(2)}) copy-start(f32[2,8]{1,0:T(2,128)} %param.24) | copy-start | bytes 196
  98.4 7.1 %copy-start.1 = (f32[1,8,128,128]{3,2,1,0:T(8,128)S(1)}, f32[1,8,128,128]{3,2,1,0:T(8,128)}, u32[]{:S(2)}) copy-start(f32[1,8,128,128]{3,2,1,0:T(8,128)} %param.21) | copy-start | bytes 1572868
  108.4 7.6 %copy-start.6 = (f32[1,8,128,128]{3,2,1,0:T(8,128)S(1)}, f32[1,8,128,128]{3,2,1,0:T(8,128)}, u32[]{:S(2)}) copy-start(f32[1,8,128,128]{3,2,1,0:T(8,128)} %param.22) | copy-start | bytes 1572868
  112.8 24.9 %collective-permute-start.4 = (f32[64,4,8,128]{3,2,1,0:T(8,128)}, f32[64,4,8,128]{3,2,1,0:T(8,128)S(1)}, u32[]{:S(2)}, u32[]{:S(2)}) collective-permute-start(f32[64,4,8,128]{3,2,1,0:T(8,128)} %all-to-all-done), channel_id=1, source_target_pairs={{0,64},{64,0},{1,65},{65,1},{2,66},{66,2},{3,67},{67,3},{4,68},{68... | collective-permute-start | bytes 3145736 | tf_op jit(solution)/shard_map/ppermute | solution.py:35
  139.0 3.3 copy-start.5
  139.0 3.3 copy-start.10
  139.1 3.2 copy-start.11
  313.3 7.5 %copy-start.2 = (f32[8,16384]{1,0:T(8,128)S(1)}, f32[8,16384]{1,0:T(8,128)}, u32[]{:S(2)}) copy-start(f32[8,16384]{1,0:T(8,128)} %get-tuple-element.420) | copy-start | bytes 1572868
  314.9 18.3 %all-to-all-start.1 = ((bf16[64,4,8,128]{3,1,2,0:T(4,128)(2,1)}), bf16[64,4,8,128]{3,1,2,0:T(4,128)(2,1)}, u32[]{:S(2)}, u32[]{:S(2)}) async-start(bf16[64,4,8,128]{3,1,2,0:T(4,128)(2,1)} %copy.144), calls=%async_computation.1 | async-start | bytes 1048576 | tf_op jit(solution)/shard_map/all_to_all | solution.py:70
  320.7 218.4 %all-reduce.3.cloned.1.call-start = ((), (), s32[]{:S(2)}) async-start(), calls=%async_computation.2 | async-start | bytes 524288 | tf_op jit(solution)/shard_map/psum | solution.py:234
  333.2 207.6 %collective-permute-start.9 = (bf16[64,4,8,128]{3,1,2,0:T(4,128)(2,1)}, bf16[64,4,8,128]{3,1,2,0:T(4,128)(2,1)}, u32[]{:S(2)}, u32[]{:S(2)}) collective-permute-start(bf16[64,4,8,128]{3,1,2,0:T(4,128)(2,1)} %all-to-all-done.1), channel_id=1, source_target_pairs={{0,64},{64,0},{1,65},{65,1},{2,66},{66,2},{3,67},{67,3},{4,68},{68... | collective-permute-start | bytes 1572872 | tf_op jit(solution)/shard_map/ppermute | solution.py:35
  335.4 213.3 %collective-permute-start.7 = (f32[8,1,128]{1,2,0:T(8,128)}, f32[8,1,128]{1,2,0:T(8,128)}, u32[]{:S(2)}, u32[]{:S(2)}) collective-permute-start(f32[8,1,128]{1,2,0:T(8,128)} %get-tuple-element.623), channel_id=1, source_target_pairs={{0,16},{16,32},{32,48},{1,17},{17,33},{33,49},{2,18},{18,34},{34,5... | collective-permute-start | bytes 12296 | tf_op jit(solution)/shard_map/ppermute | solution.py:19
  395.0 8.7 %collective-permute-start.8 = (f32[8,1,128]{1,2,0:T(8,128)}, f32[8,1,128]{1,2,0:T(8,128)S(1)}, u32[]{:S(2)}, u32[]{:S(2)}) collective-permute-start(f32[8,1,128]{1,2,0:T(8,128)} %get-tuple-element.624), channel_id=1, source_target_pairs={{16,0},{32,16},{48,32},{17,1},{33,17},{49,33},{18,2},{34,18},{50,3... | collective-permute-start | bytes 12296 | tf_op jit(solution)/shard_map/ppermute | solution.py:21
  396.9 151.8 %collective-permute-start.5 = (f32[8,128,1]{1,2,0:T(1,128)S(1)}, f32[8,128,1]{1,2,0:T(1,128)S(1)}, u32[]{:S(2)}, u32[]{:S(2)}) collective-permute-start(f32[8,128,1]{1,2,0:T(1,128)S(1)} %get-tuple-element.621), channel_id=1, source_target_pairs={{1,0},{2,1},{3,2},{4,3},{5,4},{6,5},{7,6},{8,7},{9,8},{10,9},{11,1... | collective-permute-start | bytes 12296 | tf_op jit(solution)/shard_map/ppermute | solution.py:21
  399.7 149.0 %collective-permute-start.6 = (f32[8,128,1]{1,2,0:T(1,128)S(1)}, f32[8,128,1]{1,2,0:T(1,128)S(1)}, u32[]{:S(2)}, u32[]{:S(2)}) collective-permute-start(f32[8,128,1]{1,2,0:T(1,128)S(1)} %get-tuple-element.622), channel_id=1, source_target_pairs={{0,1},{1,2},{2,3},{3,4},{4,5},{5,6},{6,7},{7,8},{8,9},{9,10},{10,1... | collective-permute-start | bytes 12296 | tf_op jit(solution)/shard_map/ppermute | solution.py:19
  (51 other events, 76.7 us)
Sparse Core Ops, SparseCore 0:
  396.5 142.6 all-reduce.2
where the time goes:
time: 561 us; the launch traced here: 559 us
  blocking collectives  177 us (32%)
  waiting for transfers between devices  162 us (29%)
  matrix products  115 us (20%)
  starting transfers between devices  36.5 us (7%)
  local copies, waits for them, and re-layouts  30.4 us (5%)
  other arithmetic  22.1 us (4%)
  between operations  14.6 us (3%)
    psum x1, waiting for transfers between devices, shards(): lax.psum((grad_first, bias_first, grad_second, bias_second, grad_third, b...  132 us
    all_gather x2, blocking collectives, laplace(): whole_row = lax.all_gather(top_row, 'gx', axis=1, tiled=True)  113 us
    psum x1, blocking collectives, shards(): lax.psum((grad_first, bias_first, grad_second, bias_second, grad_third, b...  64 us
    dot_general x8, matrix products, advance(): jnp.einsum('ho,on->hn', w_out, flux_cot, preferred_element_type=jnp.float32)  20.7 us
    ppermute x2, waiting for transfers between devices, partner(): return lax.ppermute(block, axis, route)  20.2 us
    dot_general x8, matrix products, advance(): jnp.einsum('hk,hn->kn', w_mid, hidden_first, preferred_element_type=jnp.f...  19.1 us
    dot_general x8, matrix products, advance(): jnp.dot(couple, fluxes, precision=PRECISE)  14.6 us
    ppermute x4, starting transfers between devices, extended(): lax.ppermute(head, axis, [((i + 1) % count, i) for i in range(ends)])  11.7 us
  transfers between devices with their start and end apart: 13, of which 3 were waited for; matrix products, arithmetic and copies ran while one was open for 9% of the time, Pallas kernels for 0%

commit v1 on v0

v1 whole, which is shorter than its diff:
```python
import jax
import jax.numpy as jnp
from jax import lax
from jax.experimental import pallas as pl
from jax.experimental.pallas import tpu as pltpu
from jax.sharding import PartitionSpec as P

MESH = pl.DeviceIdType.MESH
F32 = jnp.float32
BF16 = jnp.bfloat16
ENTRIES = 20
SLOTS = 4
TILE = 128
CH = 8
HID = 256
CHUNK = 4
PIECE = 40
NT = (((1,), (1,)), ((), ()))


def here():
    return lax.axis_index("comp"), lax.axis_index("gy"), lax.axis_index("gx")


def entry(n, i, j):
    top = i // 3
    if n < 15:
        row = top + n // 5
        shift = n % 5 - 2
        col = (j + shift + 16) % 16
        place = (i - row // 3) * 5 + 2 - shift
        return jnp.int32(1), row, col, place
    low = 1 - (i + 3) // 4
    middle = 1 - low - top
    shift, turn = n - 17, n - 16
    col = (middle * (j + shift) + (1 - middle) * (15 - j + turn) + 32) % 16
    apart = ((col - j + 18) % 16 + 11) // 16
    valid = middle + (top * apart if n < 18 else 0)
    place = middle * (i * 5 + 2 - shift) + (1 - middle) * n
    place = place - 5 * middle
    return valid, jnp.int32(3), col, place


def halo_peers(c, i, j):
    return (
        (jnp.int32(1), (c, i, (j + 15) % 16)),
        (jnp.int32(1), (c, i, (j + 1) % 16)),
        ((i + 3) // 4, (c, (i + 3) % 4, j)),
        (1 - i // 3, (c, (i + 1) % 4, j)),
        (c * (i // 3), (c, i, 15 - j)),
    )


def signal_to(barrier, device):
    pl.semaphore_signal(barrier, inc=1, device_id=device, device_id_type=MESH)


def greet(barrier, c, i, j):
    expected = jnp.int32(0)
    for n in range(ENTRIES):
        valid, row, col, _ = entry(n, i, j)
        expected = expected + valid
        if n < 15:
            signal_to(barrier, (1 - c, row, col))
        else:
            pl.when(valid == 1)(lambda row=row, col=col: signal_to(barrier, (1 - c, row, col)))
    for valid, device in halo_peers(c, i, j):
        expected = expected + valid
        pl.when(valid == 1)(lambda device=device: signal_to(barrier, device))
    return expected


def remote(src, dst, send, recv, device):
    return pltpu.make_async_remote_copy(
        src_ref=src, dst_ref=dst, send_sem=send, recv_sem=recv, device_id=device, device_id_type=MESH
    )


def halo_copies(c, i, j, ext, cols_out, cols_in, rows_in, send, recv):
    west, east, south, north, fold = halo_peers(c, i, j)
    return (
        (west[0], remote(cols_out.at[0], cols_in.at[1], send.at[0], recv.at[1], west[1])),
        (east[0], remote(cols_out.at[1], cols_in.at[0], send.at[1], recv.at[0], east[1])),
        (south[0], remote(ext.at[1], rows_in.at[1], send.at[2], recv.at[3], south[1])),
        (north[0], remote(ext.at[TILE], rows_in.at[0], send.at[3], recv.at[2], north[1])),
        (fold[0], remote(ext.at[TILE], rows_in.at[2], send.at[4], recv.at[4], fold[1])),
    )


def start_halo(copies):
    for valid, copy in copies:
        pl.when(valid == 1)(copy.start)


def wait_halo(c, i, j, ext, cols_out, cols_in, rows_in, send, recv):
    west, east, south, north, fold = halo_peers(c, i, j)
    from_west = remote(cols_out.at[0], cols_in.at[0], send.at[0], recv.at[0], west[1])
    from_east = remote(cols_out.at[1], cols_in.at[1], send.at[1], recv.at[1], east[1])
    from_south = remote(ext.at[1], rows_in.at[0], send.at[2], recv.at[2], south[1])
    from_north = remote(ext.at[TILE], rows_in.at[1], send.at[3], recv.at[3], north[1])
    from_fold = remote(ext.at[TILE], rows_in.at[2], send.at[4], recv.at[4], fold[1])
    from_west.wait_recv()
    from_east.wait_recv()

    @pl.when(south[0] == 1)
    def _():
        from_south.wait_recv()
        ext[0] = rows_in[0]

    @pl.when(north[0] == 1)
    def _():
        from_north.wait_recv()
        ext[TILE + 1] = rows_in[1]

    @pl.when(south[0] == 0)
    def _():
        ext[0] = jnp.zeros((CH, TILE), F32)

    @pl.when((north[0] == 0) & (fold[0] == 0))
    def _():
        ext[TILE + 1] = jnp.zeros((CH, TILE), F32)

    @pl.when(fold[0] == 1)
    def _():
        from_fold.wait_recv()
        down = lax.broadcasted_iota(jnp.int32, (TILE, TILE), 0)
        across = lax.broadcasted_iota(jnp.int32, (TILE, TILE), 1)
        turn = (down + across == TILE - 1).astype(F32)
        ext[TILE + 1] = jnp.dot(
            rows_in[2], turn, precision=lax.Precision.HIGHEST, preferred_element_type=F32
        )


def wait_halo_sent(c, i, j, ext, cols_out, cols_in, rows_in, send, recv):
    for valid, copy in halo_copies(c, i, j, ext, cols_out, cols_in, rows_in, send, recv):
        pl.when(valid == 1)(copy.wait_send)


def lanes():
    return lax.broadcasted_iota(jnp.int32, (CH, TILE), 1)


def edge_columns(ext, cols_out):
    lane = lanes()

    def step(group, carry):
        first, last = carry
        for k in range(8):
            row = group * 8 + k
            cells = ext[row + 1]
            first = jnp.where(lane == row, pltpu.roll(cells, row, 1), first)
            last = jnp.where(lane == row, pltpu.roll(cells, row + 1, 1), last)
        return first, last

    zero = jnp.zeros((CH, TILE), F32)
    first, last = lax.fori_loop(0, TILE // 8, step, (zero, zero))
    cols_out[0] = first
    cols_out[1] = last


def laplace_row(ext, cols_in, row, lane):
    cells = ext[row + 1]
    west = pltpu.roll(jnp.where(lane == TILE - 1, pltpu.roll(cols_in[0], TILE - 1 - row, 1), cells), 1, 1)
    east = pltpu.roll(jnp.where(lane == 0, pltpu.roll(cols_in[1], TILE - row, 1), cells), TILE - 1, 1)
    return east + west + ext[row] + ext[row + 2] - 4.0 * cells


def send_body(state, weights, source, count, ext, cols_in, landed,
              kernels, outgoing, cols_out, rows_in, load_sem, send_sem, recv_sem, hsend_sem, hrecv_sem):
    c, i, j = here()
    barrier = pltpu.get_barrier_semaphore()
    expected = greet(barrier, c, i, j)
    peers = [entry(n, i, j) for n in range(ENTRIES)]
    loads = []
    for n, (_, row, col, _) in enumerate(peers):
        load = pltpu.make_async_copy(weights.at[row * 16 + col], kernels.at[n], load_sem.at[n])
        load.start()
        loads.append(load)

    def turn(group, carry):
        for k in range(8):
            row = group * 8 + k
            ext[row + 1] = state[pl.ds(row, CH, stride=TILE), :]
        return carry

    lax.fori_loop(0, TILE // 8, turn, 0)
    edge_columns(ext, cols_out)
    pl.semaphore_wait(barrier, expected)
    halo = (c, i, j, ext, cols_out, cols_in, rows_in, hsend_sem, hrecv_sem)
    start_halo(halo_copies(*halo))
    sends = []
    for n, (valid, row, col, place) in enumerate(peers):
        sends.append(
            remote(outgoing.at[n], landed.at[place], send_sem.at[n], recv_sem.at[place], (1 - c, row, col))
        )
    for group in range(4):
        members = range(group * 5, group * 5 + 5)
        for n in members:
            loads[n].wait()
        for n in members:
            _, row, col, _ = peers[n]
            tile = row * 16 + col
            live = count[0, tile]
            parts = []
            for s in range(SLOTS):
                keep = (live > s).astype(F32)
                cells = (ext[source[tile, s] + 1] * keep).astype(BF16)
                parts.append(jnp.dot(cells, kernels[n, s], preferred_element_type=F32))
            outgoing[n] = jnp.concatenate(parts, axis=0).astype(BF16)
        for n in members:
            if n < 15:
                sends[n].start()
            else:
                pl.when(peers[n][0] == 1)(sends[n].start)
    wait_halo(*halo)
    for n, (valid, row, col, _) in enumerate(peers):
        arrival = remote(outgoing.at[n], landed.at[n], send_sem.at[n], recv_sem.at[n], (1 - c, row, col))
        if n < 15:
            arrival.wait_recv()
        else:
            pl.when(valid == 1)(arrival.wait_recv)

            @pl.when(valid == 0)
            def _(n=n):
                landed[n] = jnp.zeros((SLOTS * CH, TILE), BF16)

    for n, (valid, _, _, _) in enumerate(peers):
        if n < 15:
            sends[n].wait_send()
        else:
            pl.when(valid == 1)(sends[n].wait_send)
    wait_halo_sent(*halo)


def network_body(ext, cols_in, landed, target, land, rows_to, rate, couple, bias_out,
                 w_in, b_in, w_mid, b_mid, w_out, w_out_turned,
                 new_state, dm, base, going, grads,
                 remapped, other_cot, first_w, first_back, mid_turned, mid_half, out_half, mid_bias, hidden_ext, g_first, g_mid, g_out, g_bias):
    c, i, j = here()
    lane = lanes()
    peers = [entry(n, i, j) for n in range(ENTRIES)]
    remapped[...] = jnp.zeros_like(remapped)
    for n, (_, row, col, _) in enumerate(peers):
        tile = row * 16 + col
        block = landed[n].astype(F32)
        for s in range(SLOTS):
            to = rows_to[tile, s]
            remapped[to] = remapped[to] + block[s * CH:(s + 1) * CH]

    flip = c == 1
    given = w_in[...].astype(F32)
    own_w = jnp.where(flip, given[CH:], given[:CH])
    other_w = jnp.where(flip, given[:CH], given[CH:])
    bias = b_in[...]
    high = bias.astype(BF16).astype(F32)
    middle = (bias - high).astype(BF16).astype(F32)
    lower = bias - high - middle
    rows = lax.broadcasted_iota(jnp.int32, (16, HID), 0)
    extra = jnp.where(rows == 0, high, jnp.where(rows == 1, middle, jnp.where(rows == 2, lower, 0.0)))
    first_back[...] = jnp.concatenate([own_w, other_w], axis=0).astype(BF16)
    whole = jnp.concatenate([own_w, other_w, extra, jnp.zeros((TILE - 32, HID), F32)], axis=0)
    first_w[...] = (0.5 * whole.T).astype(BF16)
    mid = w_mid[...].astype(F32) * 0.5
    mid_half[...] = mid.astype(BF16)
    mid_turned[...] = mid.T.astype(BF16)
    out_half[...] = (w_out[...].astype(F32) * 0.5).astype(BF16)
    mid_bias[...] = jnp.broadcast_to(0.5 * b_mid[...], (TILE, HID)).T
    cells_count = CHUNK * TILE
    ones = (lax.broadcasted_iota(jnp.int32, (16, cells_count), 0) < 3).astype(BF16)
    hidden_ext[HID:, :] = ones
    g_first[...] = jnp.zeros_like(g_first)
    g_mid[...] = jnp.zeros_like(g_mid)
    g_out[...] = jnp.zeros_like(g_out)
    g_bias[...] = jnp.zeros_like(g_bias)
    sub = lax.broadcasted_iota(jnp.int32, (CH, TILE), 0)

    def column(scalars):
        out = jnp.zeros((CH, TILE), F32)
        for k, value in enumerate(scalars):
            out = jnp.where(sub == k, value, out)
        return out

    rates = column([rate[c, k] for k in range(CH)])
    pulls = [column([couple[c * CH + k, f] for k in range(CH)]) for f in range(4)]
    out_bias = column([bias_out[0, f] for f in range(4)])

    def step(index, carry):
        start = index * CHUNK
        blocks = []
        for k in range(CHUNK):
            blocks.append(
                jnp.concatenate([ext[start + k + 1], remapped[start + k]], axis=0).astype(BF16)
            )
        features = jnp.concatenate([jnp.concatenate(blocks, axis=1), ones], axis=0)
        half_first = jnp.dot(first_w[:, :32], features, preferred_element_type=F32)
        tan_first = jnp.tanh(half_first)
        up_first = 1.0 + tan_first
        act_first = half_first * up_first
        slope_first = up_first + act_first * (1.0 - tan_first)
        hidden_ext[:HID, :] = act_first.astype(BF16)
        half_second = jnp.dot(mid_turned[...], hidden_ext[:HID, :], preferred_element_type=F32)
        half_second = half_second + jnp.concatenate([mid_bias[...]] * CHUNK, axis=1)
        tan_second = jnp.tanh(half_second)
        up_second = 1.0 + tan_second
        act_second = half_second * up_second
        slope_second = up_second + act_second * (1.0 - tan_second)
        hidden_second = act_second.astype(BF16)
        raw = jnp.dot(w_out_turned[...], hidden_second, preferred_element_type=F32)
        misfits, cots = [], []
        for k in range(CHUNK):
            row = start + k
            wet = jnp.broadcast_to(land[pl.ds(row, 1), :].astype(F32), (CH, TILE))
            open_sea = jnp.where(flip, wet, 1.0)
            fluxes = (raw[:CH, k * TILE:(k + 1) * TILE] + out_bias) * wet
            updated = ext[row + 1] + rates * open_sea * laplace_row(ext, cols_in, row, lane)
            for f in range(4):
                updated = updated + pulls[f] * fluxes[f:f + 1]
            new_state[pl.ds(row, CH, stride=TILE), :] = updated
            misfit = updated - target[pl.ds(row, CH, stride=TILE), :]
            misfits.append(misfit)
            dm[row + 1] = misfit * open_sea
            cot = jnp.zeros((CH, TILE), F32)
            for f in range(4):
                cot = jnp.where(sub == f, jnp.sum(pulls[f] * misfit, axis=0, keepdims=True), cot)
            cot = jnp.concatenate([cot * wet, jnp.zeros((CH, TILE), F32)], axis=0).astype(BF16)
            cots.append(cot)
            g_bias[...] += cot.astype(F32)[:CH]
        flux_cot = jnp.concatenate(cots, axis=1)
        second_cot = (jnp.dot(out_half[...], flux_cot, preferred_element_type=F32) * slope_second).astype(BF16)
        first_cot = (jnp.dot(mid_half[...], second_cot, preferred_element_type=F32) * slope_first).astype(BF16)
        feature_cot = jnp.dot(first_back[...], first_cot, preferred_element_type=F32)
        g_first[...] += lax.dot_general(features, first_cot, NT, preferred_element_type=F32)
        g_mid[...] += lax.dot_general(hidden_ext[...], second_cot, NT, preferred_element_type=F32)
        g_out[...] += lax.dot_general(flux_cot, hidden_second, NT, preferred_element_type=F32)
        for k in range(CHUNK):
            piece = feature_cot[:, k * TILE:(k + 1) * TILE]
            base[start + k] = misfits[k] + piece[:CH]
            other_cot[start + k] = piece[CH:]
        return carry

    lax.fori_loop(0, TILE // CHUNK, step, 0)
    zero = jnp.zeros((CH, TILE), F32)
    dm[0] = zero
    dm[TILE + 1] = zero
    for n, (_, row, col, _) in enumerate(peers):
        tile = row * 16 + col
        going[n] = jnp.concatenate(
            [other_cot[rows_to[tile, s]] for s in range(SLOTS)], axis=0
        ).astype(BF16)
    grads[0:256] = g_mid[:HID, :TILE]
    grads[256:512] = g_mid[:HID, TILE:]
    for side in range(2):
        columns = slice(side * TILE, (side + 1) * TILE)
        at = 512 + side * 16
        grads[at:at + 8] = jnp.where(flip, g_first[8:16, columns], g_first[0:8, columns])
        grads[at + 8:at + 16] = jnp.where(flip, g_first[0:8, columns], g_first[8:16, columns])
        grads[544 + side * 8:552 + side * 8] = g_first[16:24, columns]
        grads[560 + side * 8:568 + side * 8] = g_mid[HID:HID + 8, columns]
        grads[576 + side * 8:584 + side * 8] = g_out[:CH, columns]
    grads[592:600] = g_bias[...]
    grads[600:640] = jnp.zeros((40, TILE), F32)


def return_body(going, dm_in, base, grads, weights, source, count, rate,
                adjoint, o_w_in, o_b_in, o_w_mid, o_b_mid, o_w_out, o_b_out,
                dm, kernels, back_in, cols_out, cols_in, rows_in, spread, anchor, first_in, mid_sum, second_in, total, whole,
                load_sem, send_sem, recv_sem, hsend_sem, hrecv_sem, s1, r1, s2, r2, s3, r3):
    c, i, j = here()
    lane = lanes()
    barrier = pltpu.get_barrier_semaphore()
    expected = greet(barrier, c, i, j) + 22
    me = c * 4 + i
    across = [(j + d) % 16 for d in range(1, 16)]
    along = [((me + d) % 8 // 4, (me + d) % 4) for d in range(1, 8)]
    for col in across:
        signal_to(barrier, (c, i, col))
    for other in along:
        signal_to(barrier, (*other, j))
    peers = [entry(n, i, j) for n in range(ENTRIES)]
    loads = []
    for n, (_, row, col, _) in enumerate(peers):
        load = pltpu.make_async_copy(weights.at[row * 16 + col], kernels.at[n], load_sem.at[n])
        load.start()
        loads.append(load)
    dm[...] = dm_in[...]
    edge_columns(dm, cols_out)
    pl.semaphore_wait(barrier, expected)
    halo = (c, i, j, dm, cols_out, cols_in, rows_in, hsend_sem, hrecv_sem)
    phase1 = [
        remote(grads.at[col], first_in.at[d], s1.at[d], r1.at[d], (c, i, col)) for d, col in enumerate(across)
    ]
    for copy in phase1:
        copy.start()
    start_halo(halo_copies(*halo))
    sends = []
    for n, (valid, row, col, place) in enumerate(peers):
        copy = remote(going.at[n], back_in.at[place], send_sem.at[n], recv_sem.at[place], (1 - c, row, col))
        sends.append(copy)
        if n < 15:
            copy.start()
        else:
            pl.when(valid == 1)(copy.start)

    for n, (_, row, col, _) in enumerate(peers):
        tile = row * 16 + col
        live = count[0, tile]
        used = peers[n][0]
        for s in range(SLOTS):
            at = source[tile, s]
            keep = (live > s).astype(F32) * used.astype(F32)
            anchor[pl.ds(n * SLOTS + s, 1), :] = (lane[:1] == at).astype(F32) * keep
    anchor[80:, :] = jnp.zeros((TILE - 80, TILE), F32)
    turned = anchor[...].T[:, :80].astype(BF16)
    both = jnp.concatenate([turned, turned], axis=1)

    for copy in phase1:
        copy.wait_recv()
    partial = grads[j]
    for d in range(15):
        partial = partial + first_in[d]
    mid_sum[...] = partial
    phase2 = [
        remote(mid_sum, second_in.at[d], s2.at[d], r2.at[d], (*other, j)) for d, other in enumerate(along)
    ]
    for copy in phase2:
        copy.start()

    wait_halo(*halo)
    sub = lax.broadcasted_iota(jnp.int32, (CH, TILE), 0)
    rates = jnp.zeros((CH, TILE), F32)
    for k in range(CH):
        rates = jnp.where(sub == k, rate[c, k], rates)

    def step(group, carry):
        for k in range(8):
            row = group * 8 + k
            adjoint[pl.ds(row, CH, stride=TILE), :] = base[row] + rates * laplace_row(dm, cols_in, row, lane)
        return carry

    lax.fori_loop(0, TILE // 8, step, 0)

    for copy in phase2:
        copy.wait_recv()
    partial = mid_sum[...]
    for d in range(7):
        partial = partial + second_in[d]
    total[...] = partial
    whole[j] = partial
    phase3 = [
        remote(total, whole.at[j], s3.at[d], r3.at[d], (c, i, col)) for d, col in enumerate(across)
    ]
    for copy in phase3:
        copy.start()

    for n, (valid, row, col, _) in enumerate(peers):
        arrival = remote(going.at[n], back_in.at[n], send_sem.at[n], recv_sem.at[n], (1 - c, row, col))
        if n < 15:
            arrival.wait_recv()
        else:
            pl.when(valid == 1)(arrival.wait_recv)

            @pl.when(valid == 0)
            def _(n=n):
                back_in[n] = jnp.zeros((SLOTS * CH, TILE), BF16)

    for n in range(ENTRIES):
        loads[n].wait()
    for n in range(ENTRIES):
        made = lax.dot_general(
            back_in[n], kernels[n].reshape(SLOTS * TILE, TILE), NT, preferred_element_type=F32
        )
        for s in range(SLOTS):
            spread[pl.ds(n * SLOTS + s, CH, stride=80), :] = made[s * CH:(s + 1) * CH, s * TILE:(s + 1) * TILE]
    for ch in range(CH):
        cells = spread[ch * 80:(ch + 1) * 80, :]
        high = cells.astype(BF16)
        low = (cells - high.astype(F32)).astype(BF16)
        adjoint[ch * TILE:(ch + 1) * TILE, :] += jnp.dot(
            both, jnp.concatenate([high, low], axis=0), preferred_element_type=F32
        )

    for d in range(15):
        remote(total, whole.at[(j + 15 - d) % 16], s3.at[d], r3.at[d], (c, i, across[d])).wait_recv()
    flat = whole[...].reshape(16 * PIECE, TILE) * (1.0 / 1048576.0)
    for side in range(2):
        columns = slice(side * TILE, (side + 1) * TILE)
        o_w_mid[:, columns] = flat[side * HID:(side + 1) * HID]
        o_w_in[:, columns] = flat[512 + side * 16:528 + side * 16]
        o_b_in[:, columns] = flat[544 + side * 8:545 + side * 8]
        o_b_mid[:, columns] = flat[560 + side * 8:561 + side * 8]
        o_w_out[:, columns] = flat[576 + side * 8:584 + side * 8]
    o_b_out[...] = jnp.broadcast_to(jnp.sum(flat[592:600], axis=1, keepdims=True), (CH, TILE))
    for n, (valid, _, _, _) in enumerate(peers):
        if n < 15:
            sends[n].wait_send()
        else:
            pl.when(valid == 1)(sends[n].wait_send)
    wait_halo_sent(*halo)
    for copy in phase1 + phase2 + phase3:
        copy.wait_send()


VM = pl.BlockSpec(memory_space=pltpu.VMEM)
SM = pl.BlockSpec(memory_space=pltpu.SMEM)
ANY = pl.BlockSpec(memory_space=pl.ANY)
DMA = pltpu.SemaphoreType.DMA


def arr(shape, dtype=F32):
    return jax.ShapeDtypeStruct(shape, dtype)


def shards(state, target, land_mask, diffusivity, coupling, w_in, b_in, w_mid, b_mid, w_out, b_out,
           remap_weight, remap_source, remap_target, remap_count):
    weights = remap_weight.reshape(64, SLOTS, TILE, TILE)
    source = remap_source.reshape(64, SLOTS)
    rows_to = remap_target.reshape(64, SLOTS)
    count = remap_count.reshape(1, 64)
    cells = state.reshape(CH * TILE, TILE)
    goal = target.reshape(CH * TILE, TILE)
    land = land_mask.reshape(TILE, TILE)
    ext, cols_in, landed = pl.pallas_call(
        send_body,
        out_shape=(arr((TILE + 2, CH, TILE)), arr((2, CH, TILE)), arr((ENTRIES, SLOTS * CH, TILE), BF16)),
        in_specs=[VM, ANY, SM, SM],
        out_specs=(VM, VM, VM),
        scratch_shapes=[
            pltpu.VMEM((ENTRIES, SLOTS, TILE, TILE), BF16),
            pltpu.VMEM((ENTRIES, SLOTS * CH, TILE), BF16),
            pltpu.VMEM((2, CH, TILE), F32),
            pltpu.VMEM((3, CH, TILE), F32),
            DMA((ENTRIES,)), DMA((ENTRIES,)), DMA((ENTRIES,)), DMA((5,)), DMA((5,)),
        ],
        compiler_params=pltpu.CompilerParams(
            collective_id=0, has_side_effects=True, vmem_limit_bytes=24 << 20
        ),
        name="remap_send",
    )(cells, weights, source, count)

    new_state, dm, base, going, grads = pl.pallas_call(
        network_body,
        out_shape=(
            arr((CH * TILE, TILE)),
            arr((TILE + 2, CH, TILE)),
            arr((TILE, CH, TILE)),
            arr((ENTRIES, SLOTS * CH, TILE), BF16),
            arr((16 * PIECE, TILE)),
        ),
        in_specs=[VM] * 5 + [SM] * 4 + [VM] * 6,
        out_specs=(VM,) * 5,
        scratch_shapes=[
            pltpu.VMEM((TILE, CH, TILE), F32),
            pltpu.VMEM((TILE, CH, TILE), F32),
            pltpu.VMEM((HID, TILE), BF16),
            pltpu.VMEM((16, HID), BF16),
            pltpu.VMEM((HID, HID), BF16),
            pltpu.VMEM((HID, HID), BF16),
            pltpu.VMEM((HID, 16), BF16),
            pltpu.VMEM((HID, TILE), F32),
            pltpu.VMEM((HID + 16, CHUNK * TILE), BF16),
            pltpu.VMEM((32, HID), F32),
            pltpu.VMEM((HID + 16, HID), F32),
            pltpu.VMEM((16, HID), F32),
            pltpu.VMEM((CH, TILE), F32),
        ],
        compiler_params=pltpu.CompilerParams(vmem_limit_bytes=32 << 20),
        name="network",
    )(
        ext, cols_in, landed, goal, land, rows_to, diffusivity, coupling.reshape(2 * CH, 4), b_out.reshape(1, 4),
        w_in, b_in.reshape(1, HID), w_mid, b_mid.reshape(1, HID),
        jnp.pad(w_out, ((0, 0), (0, 12))), jnp.pad(w_out.T, ((0, 12), (0, 0))),
    )

    adjoint, g_w_in, g_b_in, g_w_mid, g_b_mid, g_w_out, g_b_out = pl.pallas_call(
        return_body,
        out_shape=(
            arr((CH * TILE, TILE)), arr((16, HID)), arr((1, HID)), arr((HID, HID)), arr((1, HID)),
            arr((CH, HID)), arr((CH, TILE)),
        ),
        in_specs=[VM] * 4 + [ANY] + [SM] * 3,
        out_specs=(VM,) * 7,
        scratch_shapes=[
            pltpu.VMEM((TILE + 2, CH, TILE), F32),
            pltpu.VMEM((ENTRIES, SLOTS, TILE, TILE), BF16),
            pltpu.VMEM((ENTRIES, SLOTS * CH, TILE), BF16),
            pltpu.VMEM((2, CH, TILE), F32),
            pltpu.VMEM((2, CH, TILE), F32),
            pltpu.VMEM((3, CH, TILE), F32),
            pltpu.VMEM((ENTRIES * SLOTS * CH, TILE), F32),
            pltpu.VMEM((TILE, TILE), F32),
            pltpu.VMEM((15, PIECE, TILE), F32),
            pltpu.VMEM((PIECE, TILE), F32),
            pltpu.VMEM((7, PIECE, TILE), F32),
            pltpu.VMEM((PIECE, TILE), F32),
            pltpu.VMEM((16, PIECE, TILE), F32),
            DMA((ENTRIES,)), DMA((ENTRIES,)), DMA((ENTRIES,)), DMA((5,)), DMA((5,)),
            DMA((15,)), DMA((15,)), DMA((7,)), DMA((7,)), DMA((15,)), DMA((15,)),
        ],
        compiler_params=pltpu.CompilerParams(
            collective_id=1, has_side_effects=True, vmem_limit_bytes=32 << 20
        ),
        name="remap_return",
    )(going, dm, base, grads.reshape(16, PIECE, TILE), weights, source, count, diffusivity)
    return (
        new_state.reshape(1, CH, TILE, TILE),
        adjoint.reshape(1, CH, TILE, TILE),
        g_w_in,
        g_b_in.reshape(HID),
        g_w_mid,
        g_b_mid.reshape(HID),
        g_w_out[:4].T,
        g_b_out[:4, 0],
    )


def solution(mesh):
    tiles = P("comp", None, "gy", "gx")
    pairs = P("comp", "gy", "gx")
    return jax.shard_map(
        shards,
        mesh=mesh,
        in_specs=(tiles, tiles, pairs) + (P(),) * 8 + (pairs,) * 4,
        out_specs=(tiles, tiles) + (P(),) * 6,
        check_vma=False,
    )
```

time: 561 us -> 104 us (0.19)
  blocking collectives: 177 us -> 0 us
  waiting for transfers between devices: 162 us -> 0 us
  matrix products: 115 us -> 0 us
  Pallas kernels: 0 us -> 89.2 us
  starting transfers between devices: 36.5 us -> 0 us
  other arithmetic: 22.1 us -> 0 us
  local copies, waits for them, and re-layouts: 30.4 us -> 13.5 us
  between operations: 14.6 us -> 0.8 us
    psum x1 -> x0, waiting for transfers between devices: 132 us -> none  [shards(): lax.psum((grad_first, bias_first, grad_second, bias_second, grad_third, b...]
    dot_general x93 -> x0, matrix products: 115 us -> none  [the longest x8 20.7 us: advance(): jnp.einsum('ho,on->hn', w_out, flux_cot, preferred_element_type=jnp.float32)]
    all_gather x2 -> x0, blocking collectives: 113 us -> none  [laplace(): whole_row = lax.all_gather(top_row, 'gx', axis=1, tiled=True)]
    pallas_call x0 -> x3, Pallas kernels: none -> 89.2 us  [the longest x1 45.6 us: shards(): pl.pallas_call(network_body, out_shape=(arr((CH * TILE, TILE)), arr((TILE...]
    psum x1 -> x0, blocking collectives: 64 us -> none  [shards(): lax.psum((grad_first, bias_first, grad_second, bias_second, grad_third, b...]
    ppermute x10 -> x0, starting transfers between devices: 22.5 us -> none  [the longest x4 11.7 us: extended(): lax.ppermute(head, axis, [((i + 1) % count, i) for i in range(ends)])]
    ppermute x10 -> x0, waiting for transfers between devices: 20.2 us -> none  [the longest x2 20.2 us: partner(): return lax.ppermute(block, axis, route)]
    all_to_all x2 -> x0, starting transfers between devices: 14 us -> none  [the longest x1 8.14 us: forward_route(): lax.all_to_all(outgoing, ('gy', 'gx'), split_axis=0, concat_axis=0, tiled...]
  transfers between devices with their start and end apart: 13 -> 0, of which waited for: 3 -> 0; matrix products, arithmetic and copies ran while one was open for 9% -> 0% of each run, Pallas kernels for 0% -> 0%
where the time goes in v1:
time: 104 us; the launch traced here: 103 us
  Pallas kernels  89.2 us (86%)
  local copies, waits for them, and re-layouts  13.5 us (13%)
    pallas_call x1, Pallas kernels, shards(): pl.pallas_call(network_body, out_shape=(arr((CH * TILE, TILE)), arr((TILE...  45.6 us
    pallas_call x1, Pallas kernels, shards(): pl.pallas_call(return_body, out_shape=(arr((CH * TILE, TILE)), arr((16, H...  24.5 us
    pallas_call x1, Pallas kernels, shards(): pl.pallas_call(send_body, out_shape=(arr((TILE + 2, CH, TILE)), arr((2, C...  19 us
    unnamed x32, local copies, waits for them, and re-layouts  10.7 us

profile of v1, /device:TPU:0, one launch (start us, length us, event | category | flops | bytes accessed | tf_op | source)
XLA Modules:
  0.0 103.5 jit_solution(15937785680097492395)
XLA Ops:
  0.6 0.0 copy-start.7
  0.6 0.0 copy-start.11
  0.7 0.0 copy-start.10
  0.7 0.0 copy-start.4
  0.7 0.0 copy-start.9
  0.7 0.9 copy.33
  1.6 0.7 pad.9.w_out_turned
  2.3 0.8 copy.28
  3.0 0.8 copy.29
  3.8 0.8 copy.31
  4.6 0.0 copy-start
  4.7 3.4 %copy-done = bf16[1,1,1,64,4,128,128]{6,5,4,3,2,1,0:T(8,128)(2,1)S(1)} copy-done((bf16[1,1,1,64,4,128,128]{6,5,4,3,2,1,0:T(8,128)(2,1)S(1)}, bf16[1,1,1,64,4,128,128]{6,5,4,3,2,1,0:T(8,128)(2,1)}, u32[]{:S(2)}) %copy-start) | copy-done | bytes 8388632
  8.0 1.0 %copy-done.2 = f32[1,8,128,128]{3,2,1,0:T(8,128)S(1)} copy-done((f32[1,8,128,128]{3,2,1,0:T(8,128)S(1)}, f32[1,8,128,128]{3,2,1,0:T(8,128)}, u32[]{:S(2)}) %copy-start.2) | copy-done | bytes 524312
  9.1 0.7 copy-done.8
  9.7 19.0 %remap_send.1 = (f32[130,8,128]{2,1,0:T(8,128)S(1)}, f32[2,8,128]{2,1,0:T(8,128)S(1)}, bf16[20,32,128]{2,1,0:T(8,128)(2,1)S(1)}) custom-call(f32[1024,128]{1,0:T(8,128)S(1)} %bitcast.21, bf16[64,4,128,128]{3,2,1,0:T(8,128)(2,1)S(1)} %bitcast.19, s32[64,4]{1,0:T(8,128)S(1)} %bitcast.25, s32[1,64]{1,0:T(1,128)S(1)} %bitcast.30), custom_call_target="tpu_custom_call" | custom-call | tf_op jit(solution)/shard_map/remap_send/pallas_call | solution.py:522
  28.9 45.6 %network.1 = (f32[1024,128]{1,0:T(8,128)}, f32[130,8,128]{2,1,0:T(8,128)S(1)}, f32[128,8,128]{2,1,0:T(8,128)S(1)}, bf16[20,32,128]{2,1,0:T(8,128)(2,1)S(1)}, f32[640,128]{1,0:T(8,128)S(1)}) custom-call(f32[130,8,128]{2,1,0:T(8,128)S(1)} %get-tuple-element.23.ext, f32[2,8,128]{2,1,0:T(8,128)S(1)} %get-tuple-element.24.cols_in, ...), custom_call_target="tpu_custom_call" | custom-call | tf_op jit(solution)/shard_map/network/pallas_call | solution.py:540
  74.5 24.5 %remap_return.1 = (f32[1024,128]{1,0:T(8,128)S(1)}, f32[16,256]{1,0:T(8,128)S(1)}, f32[1,256]{1,0:T(1,128)S(1)}, f32[256,256]{1,0:T(8,128)S(1)}, f32[1,256]{1,0:...) custom-call(bf16[20,32,128]{2,1,0:T(8,128)(2,1)S(1)} %get-tuple-element.27.going, ...), custom_call_target="tpu_custom_call" | custom-call | tf_op jit(solution)/shard_map/remap_return/pallas_call | solution.py:574
  99.0 0.6 slice_reduce_fusion
  99.7 0.6 slice_bitcast_fusion
  100.3 0.8 copy.40
  101.1 0.6 copy.41
  101.7 0.6 copy.42
  102.2 0.7 copy.43
  102.9 0.6 copy.44
  (16 shorter events, 0.0 us)
Async XLA Ops:
  0.6 28.1 %copy-start.7 = (f32[2,8]{1,0:T(2,128)S(1)}, f32[2,8]{1,0:T(2,128)}, u32[]{:S(2)}) copy-start(f32[2,8]{1,0:T(2,128)} %rate.3) | copy-start | bytes 196
  0.6 28.1 %copy-start.11 = (f32[4]{0:T(128)S(1)}, f32[4]{0:T(128)}, u32[]{:S(2)}) copy-start(f32[4]{0:T(128)} %param.25) | copy-start | bytes 52
  0.7 28.1 %copy-start.10 = (f32[256]{0:T(256)S(1)}, f32[256]{0:T(256)}, u32[]{:S(2)}) copy-start(f32[256]{0:T(256)} %param.23) | copy-start | bytes 3076
  0.7 28.1 %copy-start.4 = (bf16[256,256]{1,0:T(8,128)(2,1)S(1)}, bf16[256,256]{1,0:T(8,128)(2,1)}, u32[]{:S(2)}) copy-start(bf16[256,256]{1,0:T(8,128)(2,1)} %w_mid.1) | copy-start | bytes 393220
  0.7 28.1 %copy-start.9 = (f32[256]{0:T(256)S(1)}, f32[256]{0:T(256)}, u32[]{:S(2)}) copy-start(f32[256]{0:T(256)} %param.21) | copy-start | bytes 3076
  0.7 28.1 %copy-start.6 = (bf16[16,256]{1,0:T(8,128)(2,1)S(1)}, bf16[16,256]{1,0:T(8,128)(2,1)}, u32[]{:S(2)}) copy-start(bf16[16,256]{1,0:T(8,128)(2,1)} %w_in.1) | copy-start | bytes 24580
  0.7 28.1 %copy-start.5 = (s32[1,128,128]{2,1,0:T(8,128)S(1)}, s32[1,128,128]{2,1,0:T(8,128)}, u32[]{:S(2)}) copy-start(s32[1,128,128]{2,1,0:T(8,128)} %param.17) | copy-start | bytes 196612
  4.6 3.4 %copy-start = (bf16[1,1,1,64,4,128,128]{6,5,4,3,2,1,0:T(8,128)(2,1)S(1)}, bf16[1,1,1,64,4,128,128]{6,5,4,3,2,1,0:T(8,128)(2,1)}, u32[]{:S(2)}) copy-start(bf16[1,1,1,64,4,128,128]{6,5,4,3,2,1,0:T(8,128)(2,1)} %param.26) | copy-start | bytes 25165828
  8.0 1.0 %copy-start.2 = (f32[1,8,128,128]{3,2,1,0:T(8,128)S(1)}, f32[1,8,128,128]{3,2,1,0:T(8,128)}, u32[]{:S(2)}) copy-start(f32[1,8,128,128]{3,2,1,0:T(8,128)} %param.15) | copy-start | bytes 1572868
  9.1 0.7 copy-start.8
  9.7 19.1 %copy-start.3 = (f32[1,8,128,128]{3,2,1,0:T(8,128)S(1)}, f32[1,8,128,128]{3,2,1,0:T(8,128)}, u32[]{:S(2)}) copy-start(f32[1,8,128,128]{3,2,1,0:T(8,128)} %param.16) | copy-start | bytes 1572868
  9.7 64.8 %copy-start.1 = (bf16[1,1,1,64,4,128,128]{6,5,4,3,2,1,0:T(8,128)(2,1)S(1)}, bf16[1,1,1,64,4,128,128]{6,5,4,3,2,1,0:T(8,128)(2,1)}, u32[]{:S(2)}) copy-start(bf16[1,1,1,64,4,128,128]{6,5,4,3,2,1,0:T(8,128)(2,1)} %param.26) | copy-start | bytes 25165828

commit v2 on v1

--- a/solution.py
+++ b/solution.py
@@ -13,8 +13,9 @@
 TILE = 128
 CH = 8
 HID = 256
-CHUNK = 4
+CHUNK = 8
 PIECE = 40
+WIDE = 256
 NT = (((1,), (1,)), ((), ()))
 
 
@@ -165,9 +166,15 @@
     return east + west + ext[row] + ext[row + 2] - 4.0 * cells
 
 
-def send_body(state, weights, source, count, ext, cols_in, landed,
-              kernels, outgoing, cols_out, rows_in, load_sem, send_sem, recv_sem, hsend_sem, hrecv_sem):
+def send_body(state_in, weights, source_in, count_in, ext, cols_in, landed,
+              state, source, count, kernels, outgoing, cols_out, rows_in, load_sem, send_sem, recv_sem, hsend_sem, hrecv_sem, in_sem):
     c, i, j = here()
+    firsts = [
+        pltpu.make_async_copy(given, held, in_sem.at[k])
+        for k, (given, held) in enumerate(((state_in, state), (source_in, source), (count_in, count)))
+    ]
+    for load in firsts:
+        load.start()
     barrier = pltpu.get_barrier_semaphore()
     expected = greet(barrier, c, i, j)
     peers = [entry(n, i, j) for n in range(ENTRIES)]
@@ -176,6 +183,8 @@
         load = pltpu.make_async_copy(weights.at[row * 16 + col], kernels.at[n], load_sem.at[n])
         load.start()
         loads.append(load)
+    for load in firsts:
+        load.wait()
 
     def turn(group, carry):
         for k in range(8):
@@ -204,7 +213,7 @@
             parts = []
             for s in range(SLOTS):
                 keep = (live > s).astype(F32)
-                cells = (ext[source[tile, s] + 1] * keep).astype(BF16)
+                cells = (ext[source[s, tile] + 1] * keep).astype(BF16)
                 parts.append(jnp.dot(cells, kernels[n, s], preferred_element_type=F32))
             outgoing[n] = jnp.concatenate(parts, axis=0).astype(BF16)
         for n in members:
@@ -233,9 +242,9 @@
 
 
 def network_body(ext, cols_in, landed, target, land, rows_to, rate, couple, bias_out,
-                 w_in, b_in, w_mid, b_mid, w_out, w_out_turned,
+                 w_in, b_in, w_mid, b_mid, w_out,
                  new_state, dm, base, going, grads,
-                 remapped, other_cot, first_w, first_back, mid_turned, mid_half, out_half, mid_bias, hidden_ext, g_first, g_mid, g_out, g_bias):
+                 remapped, other_cot, first_w, first_back, mid_turned, mid_half, out_half, w_out_turned, mid_bias, g_first, g_mid, g_out, g_bias, *kept):
     c, i, j = here()
     lane = lanes()
     peers = [entry(n, i, j) for n in range(ENTRIES)]
@@ -244,7 +253,7 @@
         tile = row * 16 + col
         block = landed[n].astype(F32)
         for s in range(SLOTS):
-            to = rows_to[tile, s]
+            to = rows_to[s, tile]
             remapped[to] = remapped[to] + block[s * CH:(s + 1) * CH]
 
     flip = c == 1
@@ -263,11 +272,14 @@
     mid = w_mid[...].astype(F32) * 0.5
     mid_half[...] = mid.astype(BF16)
     mid_turned[...] = mid.T.astype(BF16)
-    out_half[...] = (w_out[...].astype(F32) * 0.5).astype(BF16)
+    tall = jnp.concatenate([w_out[...].astype(F32), jnp.zeros((TILE - 4, HID), F32)], axis=0)
+    w_out_turned[...] = tall[:16].astype(BF16)
+    out_half[...] = (0.5 * tall.T)[:, :16].astype(BF16)
     mid_bias[...] = jnp.broadcast_to(0.5 * b_mid[...], (TILE, HID)).T
-    cells_count = CHUNK * TILE
-    ones = (lax.broadcasted_iota(jnp.int32, (16, cells_count), 0) < 3).astype(BF16)
-    hidden_ext[HID:, :] = ones
+    ones = (lax.broadcasted_iota(jnp.int32, (16, WIDE), 0) < 3).astype(BF16)
+    for p in range(CHUNK * TILE // WIDE):
+        kept[1][HID:, p * WIDE:(p + 1) * WIDE] = ones
+        kept[10][HID:, p * WIDE:(p + 1) * WIDE] = ones
     g_first[...] = jnp.zeros_like(g_first)
     g_mid[...] = jnp.zeros_like(g_mid)
     g_out[...] = jnp.zeros_like(g_out)
@@ -281,37 +293,48 @@
         return out
 
     rates = column([rate[c, k] for k in range(CH)])
-    pulls = [column([couple[c * CH + k, f] for k in range(CH)]) for f in range(4)]
+    pulls = [column([couple[c, f, k] for k in range(CH)]) for f in range(4)]
     out_bias = column([bias_out[0, f] for f in range(4)])
 
-    def step(index, carry):
-        start = index * CHUNK
-        blocks = []
-        for k in range(CHUNK):
-            blocks.append(
-                jnp.concatenate([ext[start + k + 1], remapped[start + k]], axis=0).astype(BF16)
-            )
+    def forward(start, part, features_ref, hidden_ref, slope_one, slope_two, second_ref, raw_ref, *_):
+        span = slice(part * WIDE, (part + 1) * WIDE)
+        first_row = start + part * (WIDE // TILE)
+        blocks = [
+            jnp.concatenate([ext[first_row + k + 1], remapped[first_row + k]], axis=0).astype(BF16)
+            for k in range(WIDE // TILE)
+        ]
         features = jnp.concatenate([jnp.concatenate(blocks, axis=1), ones], axis=0)
+        features_ref[:, span] = features
         half_first = jnp.dot(first_w[:, :32], features, preferred_element_type=F32)
+        yield
         tan_first = jnp.tanh(half_first)
         up_first = 1.0 + tan_first
         act_first = half_first * up_first
-        slope_first = up_first + act_first * (1.0 - tan_first)
-        hidden_ext[:HID, :] = act_first.astype(BF16)
-        half_second = jnp.dot(mid_turned[...], hidden_ext[:HID, :], preferred_element_type=F32)
-        half_second = half_second + jnp.concatenate([mid_bias[...]] * CHUNK, axis=1)
+        slope_one[:, span] = up_first + act_first * (1.0 - tan_first)
+        hidden_first = act_first.astype(BF16)
+        hidden_ref[:HID, span] = hidden_first
+        half_second = jnp.dot(mid_turned[...], hidden_first, preferred_element_type=F32)
+        yield
+        half_second = half_second + jnp.concatenate([mid_bias[...]] * (WIDE // TILE), axis=1)
         tan_second = jnp.tanh(half_second)
         up_second = 1.0 + tan_second
         act_second = half_second * up_second
-        slope_second = up_second + act_second * (1.0 - tan_second)
+        slope_two[:, span] = up_second + act_second * (1.0 - tan_second)
         hidden_second = act_second.astype(BF16)
-        raw = jnp.dot(w_out_turned[...], hidden_second, preferred_element_type=F32)
+        second_ref[:, span] = hidden_second
+        raw_ref[:, span] = jnp.dot(w_out_turned[...], hidden_second, preferred_element_type=F32)
+        yield
+
+    def backward(start, part, features_ref, hidden_ref, slope_one, slope_two, second_ref, raw_ref, one_ref, two_ref, cot_ref):
+        span = slice(part * WIDE, (part + 1) * WIDE)
+        first_row = start + part * (WIDE // TILE)
+        raw = raw_ref[:CH, span]
         misfits, cots = [], []
-        for k in range(CHUNK):
-            row = start + k
+        for k in range(WIDE // TILE):
+            row = first_row + k
             wet = jnp.broadcast_to(land[pl.ds(row, 1), :].astype(F32), (CH, TILE))
             open_sea = jnp.where(flip, wet, 1.0)
-            fluxes = (raw[:CH, k * TILE:(k + 1) * TILE] + out_bias) * wet
+            fluxes = (raw[:, k * TILE:(k + 1) * TILE] + out_bias) * wet
             updated = ext[row + 1] + rates * open_sea * laplace_row(ext, cols_in, row, lane)
             for f in range(4):
                 updated = updated + pulls[f] * fluxes[f:f + 1]
@@ -326,26 +349,59 @@
             cots.append(cot)
             g_bias[...] += cot.astype(F32)[:CH]
         flux_cot = jnp.concatenate(cots, axis=1)
-        second_cot = (jnp.dot(out_half[...], flux_cot, preferred_element_type=F32) * slope_second).astype(BF16)
-        first_cot = (jnp.dot(mid_half[...], second_cot, preferred_element_type=F32) * slope_first).astype(BF16)
+        cot_ref[:, span] = flux_cot
+        pulled = jnp.dot(out_half[...], flux_cot, preferred_element_type=F32)
+        yield
+        second_cot = (pulled * slope_two[:, span]).astype(BF16)
+        two_ref[:, span] = second_cot
+        pulled = jnp.dot(mid_half[...], second_cot, preferred_element_type=F32)
+        yield
+        first_cot = (pulled * slope_one[:, span]).astype(BF16)
+        one_ref[:, span] = first_cot
         feature_cot = jnp.dot(first_back[...], first_cot, preferred_element_type=F32)
-        g_first[...] += lax.dot_general(features, first_cot, NT, preferred_element_type=F32)
-        g_mid[...] += lax.dot_general(hidden_ext[...], second_cot, NT, preferred_element_type=F32)
-        g_out[...] += lax.dot_general(flux_cot, hidden_second, NT, preferred_element_type=F32)
-        for k in range(CHUNK):
+        yield
+        for k in range(WIDE // TILE):
             piece = feature_cot[:, k * TILE:(k + 1) * TILE]
-            base[start + k] = misfits[k] + piece[:CH]
-            other_cot[start + k] = piece[CH:]
+            base[first_row + k] = misfits[k] + piece[:CH]
+            other_cot[first_row + k] = piece[CH:]
+
+    def gradients(features_ref, hidden_ref, slope_one, slope_two, second_ref, raw_ref, one_ref, two_ref, cot_ref):
+        g_mid[...] += lax.dot_general(hidden_ref[...], two_ref[...], NT, preferred_element_type=F32)
+        g_out[...] += lax.dot_general(cot_ref[...], second_ref[...], NT, preferred_element_type=F32)
+        g_first[...] += lax.dot_general(features_ref[...], one_ref[...], NT, preferred_element_type=F32)
+
+    def play(*chains):
+        chains = list(chains)
+        while chains:
+            chains = [chain for chain in chains if next(chain, chain) is not chain]
+
+    PARTS = CHUNK * TILE // WIDE
+    half = len(kept) // 2
+    even, odd = kept[:half], kept[half:]
+    play(*(forward(0, p, *even) for p in range(PARTS)))
+
+    def both(back_at, back, front_at, front):
+        chains = []
+        for p in range(PARTS):
+            chains.append(forward(front_at, p, *front))
+            chains.append(backward(back_at, p, *back))
+        play(*chains)
+        gradients(*back)
+
+    def step(pair, carry):
+        at = pair * (2 * CHUNK)
+        both(at, even, at + CHUNK, odd)
+        both(at + CHUNK, odd, jnp.minimum(at + 2 * CHUNK, TILE - CHUNK), even)
         return carry
 
-    lax.fori_loop(0, TILE // CHUNK, step, 0)
+    lax.fori_loop(0, TILE // (2 * CHUNK), step, 0)
     zero = jnp.zeros((CH, TILE), F32)
     dm[0] = zero
     dm[TILE + 1] = zero
     for n, (_, row, col, _) in enumerate(peers):
         tile = row * 16 + col
         going[n] = jnp.concatenate(
-            [other_cot[rows_to[tile, s]] for s in range(SLOTS)], axis=0
+            [other_cot[rows_to[s, tile]] for s in range(SLOTS)], axis=0
         ).astype(BF16)
     grads[0:256] = g_mid[:HID, :TILE]
     grads[256:512] = g_mid[:HID, TILE:]
@@ -362,8 +418,8 @@
 
 
 def return_body(going, dm_in, base, grads, weights, source, count, rate,
-                adjoint, o_w_in, o_b_in, o_w_mid, o_b_mid, o_w_out, o_b_out,
-                dm, kernels, back_in, cols_out, cols_in, rows_in, spread, anchor, first_in, mid_sum, second_in, total, whole,
+                adjoint, whole,
+                dm, kernels, back_in, cols_out, cols_in, rows_in, spread, anchor, first_in, mid_sum, second_in, total,
                 load_sem, send_sem, recv_sem, hsend_sem, hrecv_sem, s1, r1, s2, r2, s3, r3):
     c, i, j = here()
     lane = lanes()
@@ -406,7 +462,7 @@
         live = count[0, tile]
         used = peers[n][0]
         for s in range(SLOTS):
-            at = source[tile, s]
+            at = source[s, tile]
             keep = (live > s).astype(F32) * used.astype(F32)
             anchor[pl.ds(n * SLOTS + s, 1), :] = (lane[:1] == at).astype(F32) * keep
     anchor[80:, :] = jnp.zeros((TILE - 80, TILE), F32)
@@ -481,15 +537,6 @@
 
     for d in range(15):
         remote(total, whole.at[(j + 15 - d) % 16], s3.at[d], r3.at[d], (c, i, across[d])).wait_recv()
-    flat = whole[...].reshape(16 * PIECE, TILE) * (1.0 / 1048576.0)
-    for side in range(2):
-        columns = slice(side * TILE, (side + 1) * TILE)
-        o_w_mid[:, columns] = flat[side * HID:(side + 1) * HID]
-        o_w_in[:, columns] = flat[512 + side * 16:528 + side * 16]
-        o_b_in[:, columns] = flat[544 + side * 8:545 + side * 8]
-        o_b_mid[:, columns] = flat[560 + side * 8:561 + side * 8]
-        o_w_out[:, columns] = flat[576 + side * 8:584 + side * 8]
-    o_b_out[...] = jnp.broadcast_to(jnp.sum(flat[592:600], axis=1, keepdims=True), (CH, TILE))
     for n, (valid, _, _, _) in enumerate(peers):
         if n < 15:
             sends[n].wait_send()
@@ -500,9 +547,27 @@
         copy.wait_send()
 
 
+def finish_body(adjoint_in, whole, adjoint, o_w_in, o_b_in, o_w_mid, o_b_mid, o_w_out, o_b_out, sem):
+    copy = pltpu.make_async_copy(adjoint_in, adjoint, sem)
+    copy.start()
+    flat = whole[...] * (1.0 / 1048576.0)
+    for side in range(2):
+        columns = slice(side * TILE, (side + 1) * TILE)
+        o_w_mid[:, columns] = flat[side * HID:(side + 1) * HID]
+        o_w_in[:, columns] = flat[512 + side * 16:528 + side * 16]
+        o_b_in[:, columns] = flat[544 + side * 8:545 + side * 8]
+        o_b_mid[:, columns] = flat[560 + side * 8:561 + side * 8]
+        o_w_out[:, columns] = flat[576 + side * 8:580 + side * 8]
+    sums = jnp.broadcast_to(jnp.sum(flat[592:600], axis=1, keepdims=True), (CH, TILE))
+    sub = lax.broadcasted_iota(jnp.int32, (CH, TILE), 0)
+    picked = jnp.sum(jnp.where(sub == lanes(), sums, 0.0), axis=0, keepdims=True)
+    o_b_out[...] = picked[:, :4]
+    copy.wait()
+
+
 VM = pl.BlockSpec(memory_space=pltpu.VMEM)
 SM = pl.BlockSpec(memory_space=pltpu.SMEM)
-ANY = pl.BlockSpec(memory_space=pl.ANY)
+HB = pl.BlockSpec(memory_space=pltpu.HBM)
 DMA = pltpu.SemaphoreType.DMA
 
 
@@ -510,34 +575,8 @@
     return jax.ShapeDtypeStruct(shape, dtype)
 
 
-def shards(state, target, land_mask, diffusivity, coupling, w_in, b_in, w_mid, b_mid, w_out, b_out,
-           remap_weight, remap_source, remap_target, remap_count):
-    weights = remap_weight.reshape(64, SLOTS, TILE, TILE)
-    source = remap_source.reshape(64, SLOTS)
-    rows_to = remap_target.reshape(64, SLOTS)
-    count = remap_count.reshape(1, 64)
-    cells = state.reshape(CH * TILE, TILE)
-    goal = target.reshape(CH * TILE, TILE)
-    land = land_mask.reshape(TILE, TILE)
-    ext, cols_in, landed = pl.pallas_call(
-        send_body,
-        out_shape=(arr((TILE + 2, CH, TILE)), arr((2, CH, TILE)), arr((ENTRIES, SLOTS * CH, TILE), BF16)),
-        in_specs=[VM, ANY, SM, SM],
-        out_specs=(VM, VM, VM),
-        scratch_shapes=[
-            pltpu.VMEM((ENTRIES, SLOTS, TILE, TILE), BF16),
-            pltpu.VMEM((ENTRIES, SLOTS * CH, TILE), BF16),
-            pltpu.VMEM((2, CH, TILE), F32),
-            pltpu.VMEM((3, CH, TILE), F32),
-            DMA((ENTRIES,)), DMA((ENTRIES,)), DMA((ENTRIES,)), DMA((5,)), DMA((5,)),
-        ],
-        compiler_params=pltpu.CompilerParams(
-            collective_id=0, has_side_effects=True, vmem_limit_bytes=24 << 20
-        ),
-        name="remap_send",
-    )(cells, weights, source, count)
-
-    new_state, dm, base, going, grads = pl.pallas_call(
+def network_call(*args):
+    return pl.pallas_call(
         network_body,
         out_shape=(
             arr((CH * TILE, TILE)),
@@ -546,7 +585,7 @@
             arr((ENTRIES, SLOTS * CH, TILE), BF16),
             arr((16 * PIECE, TILE)),
         ),
-        in_specs=[VM] * 5 + [SM] * 4 + [VM] * 6,
+        in_specs=[VM] * 5 + [SM] * 4 + [VM] * 5,
         out_specs=(VM,) * 5,
         scratch_shapes=[
             pltpu.VMEM((TILE, CH, TILE), F32),
@@ -556,29 +595,69 @@
             pltpu.VMEM((HID, HID), BF16),
             pltpu.VMEM((HID, HID), BF16),
             pltpu.VMEM((HID, 16), BF16),
+            pltpu.VMEM((16, HID), BF16),
             pltpu.VMEM((HID, TILE), F32),
-            pltpu.VMEM((HID + 16, CHUNK * TILE), BF16),
             pltpu.VMEM((32, HID), F32),
             pltpu.VMEM((HID + 16, HID), F32),
             pltpu.VMEM((16, HID), F32),
             pltpu.VMEM((CH, TILE), F32),
+        ]
+        + [
+            pltpu.VMEM((32, CHUNK * TILE), BF16),
+            pltpu.VMEM((HID + 16, CHUNK * TILE), BF16),
+            pltpu.VMEM((HID, CHUNK * TILE), F32),
+            pltpu.VMEM((HID, CHUNK * TILE), F32),
+            pltpu.VMEM((HID, CHUNK * TILE), BF16),
+            pltpu.VMEM((16, CHUNK * TILE), F32),
+            pltpu.VMEM((HID, CHUNK * TILE), BF16),
+            pltpu.VMEM((HID, CHUNK * TILE), BF16),
+            pltpu.VMEM((16, CHUNK * TILE), BF16),
+        ] * 2,
+        compiler_params=pltpu.CompilerParams(vmem_limit_bytes=48 << 20),
+        name="network",
+    )(*args)
+
+
+def shards(state, target, land_mask, diffusivity, coupling, w_in, b_in, w_mid, b_mid, w_out, b_out,
+           remap_weight, remap_source, remap_target, remap_count):
+    weights = remap_weight.reshape(64, SLOTS, TILE, TILE)
+    source = remap_source.reshape(64, SLOTS).T
+    rows_to = remap_target.reshape(64, SLOTS).T
+    count = remap_count.reshape(1, 64)
+    cells = state.reshape(CH * TILE, TILE)
+    goal = target.reshape(CH * TILE, TILE)
+    land = land_mask.reshape(TILE, TILE)
+    ext, cols_in, landed = pl.pallas_call(
+        send_body,
+        out_shape=(arr((TILE + 2, CH, TILE)), arr((2, CH, TILE)), arr((ENTRIES, SLOTS * CH, TILE), BF16)),
+        in_specs=[HB] * 4,
+        out_specs=(VM, VM, VM),
+        scratch_shapes=[
+            pltpu.VMEM((CH * TILE, TILE), F32),
+            pltpu.SMEM((SLOTS, 64), jnp.int32),
+            pltpu.SMEM((1, 64), jnp.int32),
+            pltpu.VMEM((ENTRIES, SLOTS, TILE, TILE), BF16),
+            pltpu.VMEM((ENTRIES, SLOTS * CH, TILE), BF16),
+            pltpu.VMEM((2, CH, TILE), F32),
+            pltpu.VMEM((3, CH, TILE), F32),
+            DMA((ENTRIES,)), DMA((ENTRIES,)), DMA((ENTRIES,)), DMA((5,)), DMA((5,)), DMA((3,)),
         ],
-        compiler_params=pltpu.CompilerParams(vmem_limit_bytes=32 << 20),
-        name="network",
-    )(
-        ext, cols_in, landed, goal, land, rows_to, diffusivity, coupling.reshape(2 * CH, 4), b_out.reshape(1, 4),
-        w_in, b_in.reshape(1, HID), w_mid, b_mid.reshape(1, HID),
-        jnp.pad(w_out, ((0, 0), (0, 12))), jnp.pad(w_out.T, ((0, 12), (0, 0))),
+        compiler_params=pltpu.CompilerParams(
+            collective_id=0, has_side_effects=True, vmem_limit_bytes=24 << 20
+        ),
+        name="remap_send",
+    )(*(pltpu.with_memory_space_constraint(a, pltpu.HBM) for a in (cells, weights, source, count)))
+
+    new_state, dm, base, going, grads = network_call(
+        ext, cols_in, landed, goal, land, rows_to, diffusivity, coupling.transpose(0, 2, 1),
+        b_out.reshape(1, 4), w_in, b_in.reshape(1, HID), w_mid, b_mid.reshape(1, HID), w_out.T,
     )
 
-    adjoint, g_w_in, g_b_in, g_w_mid, g_b_mid, g_w_out, g_b_out = pl.pallas_call(
+    adjoint, whole = pl.pallas_call(
         return_body,
-        out_shape=(
-            arr((CH * TILE, TILE)), arr((16, HID)), arr((1, HID)), arr((HID, HID)), arr((1, HID)),
-            arr((CH, HID)), arr((CH, TILE)),
-        ),
-        in_specs=[VM] * 4 + [ANY] + [SM] * 3,
-        out_specs=(VM,) * 7,
+        out_shape=(arr((CH * TILE, TILE)), arr((16, PIECE, TILE))),
+        in_specs=[VM] * 4 + [HB] + [SM] * 3,
+        out_specs=(VM, VM),
         scratch_shapes=[
             pltpu.VMEM((TILE + 2, CH, TILE), F32),
             pltpu.VMEM((ENTRIES, SLOTS, TILE, TILE), BF16),
@@ -592,7 +671,6 @@
             pltpu.VMEM((PIECE, TILE), F32),
             pltpu.VMEM((7, PIECE, TILE), F32),
             pltpu.VMEM((PIECE, TILE), F32),
-            pltpu.VMEM((16, PIECE, TILE), F32),
             DMA((ENTRIES,)), DMA((ENTRIES,)), DMA((ENTRIES,)), DMA((5,)), DMA((5,)),
             DMA((15,)), DMA((15,)), DMA((7,)), DMA((7,)), DMA((15,)), DMA((15,)),
         ],
@@ -600,7 +678,21 @@
             collective_id=1, has_side_effects=True, vmem_limit_bytes=32 << 20
         ),
         name="remap_return",
-    )(going, dm, base, grads.reshape(16, PIECE, TILE), weights, source, count, diffusivity)
+    )(
+        going, dm, base, grads.reshape(16, PIECE, TILE), pltpu.with_memory_space_constraint(weights, pltpu.HBM), source, count, diffusivity
+    )
+    adjoint, g_w_in, g_b_in, g_w_mid, g_b_mid, g_w_out, g_b_out = pl.pallas_call(
+        finish_body,
+        out_shape=(
+            arr((CH * TILE, TILE)), arr((16, HID)), arr((1, HID)), arr((HID, HID)), arr((1, HID)),
+            arr((4, HID)), arr((1, 4)),
+        ),
+        in_specs=[VM, VM],
+        out_specs=(HB,) + (VM,) * 6,
+        scratch_shapes=[DMA],
+        compiler_params=pltpu.CompilerParams(vmem_limit_bytes=8 << 20),
+        name="finish",
+    )(adjoint, whole.reshape(16 * PIECE, TILE))
     return (
         new_state.reshape(1, CH, TILE, TILE),
         adjoint.reshape(1, CH, TILE, TILE),
@@ -608,8 +700,8 @@
         g_b_in.reshape(HID),
         g_w_mid,
         g_b_mid.reshape(HID),
-        g_w_out[:4].T,
-        g_b_out[:4, 0],
+        g_w_out.T,
+        g_b_out.reshape(4),
     )
 
 

time: 104 us -> 69 us (0.66)
  Pallas kernels: 89.2 us -> 67.7 us
  local copies, waits for them, and re-layouts: 13.5 us -> 0.05 us
    pallas_call x2 -> x3, Pallas kernels: 70.2 us -> 52.2 us  [the longest x1 26.7 us: network_call(): pl.pallas_call(network_body, out_shape=(arr((CH * TILE, TILE)), arr((TILE...]
    unnamed x32 -> x26, local copies, waits for them, and re-layouts: 10.7 us -> 0.05 us
    pallas_call x1, Pallas kernels: 19 us -> 15.5 us  [shards(): pl.pallas_call(send_body, out_shape=(arr((TILE + 2, CH, TILE)), arr((2, C...]
where the time goes in v2:
time: 69 us; the launch traced here: 68.6 us
  Pallas kernels  67.7 us (98%)
  between operations  0.85 us (1%)
    pallas_call x1, Pallas kernels, network_call(): pl.pallas_call(network_body, out_shape=(arr((CH * TILE, TILE)), arr((TILE...  26.7 us
    pallas_call x1, Pallas kernels, shards(): pl.pallas_call(return_body, out_shape=(arr((CH * TILE, TILE)), arr((16, P...  24 us
    pallas_call x1, Pallas kernels, shards(): pl.pallas_call(send_body, out_shape=(arr((TILE + 2, CH, TILE)), arr((2, C...  15.5 us
    pallas_call x1, Pallas kernels, shards(): pl.pallas_call(finish_body, out_shape=(arr((CH * TILE, TILE)), arr((16, H...  1.54 us

profile of v2, /device:TPU:0, one launch (start us, length us, event | category | flops | bytes accessed | tf_op | source)
XLA Modules:
  0.0 68.6 jit_solution(466024517226483024)
XLA Ops:
  0.6 0.0 copy-start.6
  0.6 0.0 copy-start.9
  0.7 0.0 copy-start.7
  0.7 0.0 copy-start.4
  0.7 0.0 copy-start.12
  0.7 0.0 copy-start.8
  0.7 0.0 copy-start.11
  0.7 0.0 copy-start.1
  0.7 0.0 copy-start.10
  0.7 0.0 copy-start.3
  0.7 0.0 copy-start.5
  0.7 0.0 copy-start.2
  0.8 0.0 copy-start
  0.8 15.5 %remap_send.1 = (f32[130,8,128]{2,1,0:T(8,128)S(1)}, f32[2,8,128]{2,1,0:T(8,128)S(1)}, bf16[20,32,128]{2,1,0:T(8,128)(2,1)S(1)}) custom-call(f32[1024,128]{1,0:T(8,128)} %bitcast.40, bf16[64,4,128,128]{3,2,1,0:T(8,128)(2,1)} %bitcast.38, s32[4,64]{1,0:T(4,128)} %bitcast.28, s32[1,64]{1,0:T(1,128)} %bitcast.33), custom_call_target="tpu_custom_call" | custom-call | tf_op jit(solution)/shard_map/remap_send/pallas_call | solution.py:630
  16.3 0.0 copy-done.6
  16.3 0.0 copy-done.7
  16.3 0.0 copy-done.12
  16.3 0.0 copy-done.8
  16.3 0.0 copy-done.11
  16.3 0.0 copy-done.1
  16.4 26.7 %network.1 = (f32[1024,128]{1,0:T(8,128)}, f32[130,8,128]{2,1,0:T(8,128)S(1)}, f32[128,8,128]{2,1,0:T(8,128)S(1)}, bf16[20,32,128]{2,1,0:T(8,128)(2,1)S(1)}, f32[640,128]{1,0:T(8,128)S(1)}) custom-call(f32[130,8,128]{2,1,0:T(8,128)S(1)} %get-tuple-element.25.ext, f32[2,8,128]{2,1,0:T(8,128)S(1)} %get-tuple-element.26.cols_in, ...), custom_call_target="tpu_custom_call" | custom-call | tf_op jit(solution)/shard_map/network/pallas_call | solution.py:579
  43.1 0.0 copy-done.4
  43.1 24.0 %remap_return.1 = (f32[1024,128]{1,0:T(8,128)S(1)}, f32[16,40,128]{2,1,0:T(8,128)S(1)}) custom-call(bf16[20,32,128]{2,1,0:T(8,128)(2,1)S(1)} %get-tuple-element.29.going, f32[130,8,128]{2,1,0:T(8,128)S(1)} %get-tuple-element.30.dm_in, f32[128,8,128]{2,1,0:T(8,128)S(1)} %get-tuple-element.31.base, f32[16,40,128]{2,1,0:T(8,128)S(1)} %bitcast.25, ...), custom_call_target="tpu_custom_call" | custom-call | tf_op jit(solution)/shard_map/remap_return/pallas_call | solution.py:656
  67.1 1.5 %finish.1 = (f32[1024,128]{1,0:T(8,128)}, f32[16,256]{1,0:T(8,128)}, f32[1,256]{1,0:T(1,128)}, f32[256,256]{1,0:T(8,128)}, f32[1,256]{1,0:T(1,128)}, /*index=5*/f32[4,256]{1,0:T(4,128)}, f32[1,4]{1,0:T(1,128)}) custom-call(f32[1024,128]{1,0:T(8,128)S(1)} %get-tuple-element.33.adjoint_in, f32[640,128]{1,0:T(8,128)S(1)} %bitcast.26), custom_call_target="tpu_custom_call" | custom-call | tf_op jit(solution)/shard_map/finish/pallas_call | solution.py:684
  (6 shorter events, 0.0 us)
Async XLA Ops:
  0.6 15.6 %copy-start.6 = (f32[2,8]{1,0:T(2,128)S(1)}, f32[2,8]{1,0:T(2,128)}, u32[]{:S(2)}) copy-start(f32[2,8]{1,0:T(2,128)} %rate.3) | copy-start | bytes 196
  0.6 42.4 %copy-start.9 = (s32[1,1,1,64]{3,2,1,0:T(1,128)S(1)}, s32[1,1,1,64]{3,2,1,0:T(1,128)}, u32[]{:S(2)}) copy-start(s32[1,1,1,64]{3,2,1,0:T(1,128)} %param.29) | copy-start | bytes 772
  0.7 15.6 %copy-start.7 = (s32[1,1,1,64,4]{3,4,2,1,0:T(4,128)S(1)}, s32[1,1,1,64,4]{3,4,2,1,0:T(4,128)}, u32[]{:S(2)}) copy-start(s32[1,1,1,64,4]{3,4,2,1,0:T(4,128)} %param.28) | copy-start | bytes 3076
  0.7 42.4 %copy-start.4 = (s32[1,1,1,64,4]{3,4,2,1,0:T(4,128)S(1)}, s32[1,1,1,64,4]{3,4,2,1,0:T(4,128)}, u32[]{:S(2)}) copy-start(s32[1,1,1,64,4]{3,4,2,1,0:T(4,128)} %param.27) | copy-start | bytes 3076
  0.7 15.6 %copy-start.12 = (f32[4]{0:T(128)S(1)}, f32[4]{0:T(128)}, u32[]{:S(2)}) copy-start(f32[4]{0:T(128)} %param.25) | copy-start | bytes 52
  0.7 15.6 %copy-start.8 = (bf16[256,4]{0,1:T(4,128)(2,1)S(1)}, bf16[256,4]{0,1:T(4,128)(2,1)}, u32[]{:S(2)}) copy-start(bf16[256,4]{0,1:T(4,128)(2,1)} %param.24) | copy-start | bytes 6148
  0.7 15.6 %copy-start.11 = (f32[256]{0:T(256)S(1)}, f32[256]{0:T(256)}, u32[]{:S(2)}) copy-start(f32[256]{0:T(256)} %param.23) | copy-start | bytes 3076
  0.7 15.6 %copy-start.1 = (bf16[256,256]{1,0:T(8,128)(2,1)S(1)}, bf16[256,256]{1,0:T(8,128)(2,1)}, u32[]{:S(2)}) copy-start(bf16[256,256]{1,0:T(8,128)(2,1)} %w_mid.1) | copy-start | bytes 393220
  0.7 15.6 %copy-start.10 = (f32[256]{0:T(256)S(1)}, f32[256]{0:T(256)}, u32[]{:S(2)}) copy-start(f32[256]{0:T(256)} %param.21) | copy-start | bytes 3076
  0.7 15.6 %copy-start.3 = (bf16[16,256]{1,0:T(8,128)(2,1)S(1)}, bf16[16,256]{1,0:T(8,128)(2,1)}, u32[]{:S(2)}) copy-start(bf16[16,256]{1,0:T(8,128)(2,1)} %w_in.1) | copy-start | bytes 24580
  0.7 15.6 %copy-start.5 = (f32[2,8,4]{1,2,0:T(4,128)S(1)}, f32[2,8,4]{1,2,0:T(4,128)}, u32[]{:S(2)}) copy-start(f32[2,8,4]{1,2,0:T(4,128)} %param.19) | copy-start | bytes 772
  0.7 15.6 %copy-start.2 = (s32[1,128,128]{2,1,0:T(8,128)S(1)}, s32[1,128,128]{2,1,0:T(8,128)}, u32[]{:S(2)}) copy-start(s32[1,128,128]{2,1,0:T(8,128)} %param.17) | copy-start | bytes 196612
  0.8 15.6 %copy-start = (f32[1,8,128,128]{3,2,1,0:T(8,128)S(1)}, f32[1,8,128,128]{3,2,1,0:T(8,128)}, u32[]{:S(2)}) copy-start(f32[1,8,128,128]{3,2,1,0:T(8,128)} %param.16) | copy-start | bytes 1572868

commit v3 on v2

--- a/solution.py
+++ b/solution.py
@@ -14,8 +14,9 @@
 CH = 8
 HID = 256
 CHUNK = 8
-PIECE = 40
+PIECE = 48
 WIDE = 256
+SPREAD = (0, 2)
 NT = (((1,), (1,)), ((), ()))
 
 
@@ -144,17 +145,14 @@
 def edge_columns(ext, cols_out):
     lane = lanes()
 
-    def step(group, carry):
-        first, last = carry
-        for k in range(8):
-            row = group * 8 + k
-            cells = ext[row + 1]
-            first = jnp.where(lane == row, pltpu.roll(cells, row, 1), first)
-            last = jnp.where(lane == row, pltpu.roll(cells, row + 1, 1), last)
-        return first, last
-
-    zero = jnp.zeros((CH, TILE), F32)
-    first, last = lax.fori_loop(0, TILE // 8, step, (zero, zero))
+    firsts, lasts = [jnp.zeros((CH, TILE), F32)] * 4, [jnp.zeros((CH, TILE), F32)] * 4
+    for row in range(TILE):
+        cells = ext[row + 1]
+        k = row % 4
+        firsts[k] = jnp.where(lane == row, pltpu.roll(cells, row, 1) if row else cells, firsts[k])
+        lasts[k] = jnp.where(lane == row, pltpu.roll(cells, row + 1, 1) if row < TILE - 1 else cells, lasts[k])
+    first = (firsts[0] + firsts[1]) + (firsts[2] + firsts[3])
+    last = (lasts[0] + lasts[1]) + (lasts[2] + lasts[3])
     cols_out[0] = first
     cols_out[1] = last
 
@@ -194,9 +192,7 @@
 
     lax.fori_loop(0, TILE // 8, turn, 0)
     edge_columns(ext, cols_out)
-    pl.semaphore_wait(barrier, expected)
     halo = (c, i, j, ext, cols_out, cols_in, rows_in, hsend_sem, hrecv_sem)
-    start_halo(halo_copies(*halo))
     sends = []
     for n, (valid, row, col, place) in enumerate(peers):
         sends.append(
@@ -216,6 +212,9 @@
                 cells = (ext[source[s, tile] + 1] * keep).astype(BF16)
                 parts.append(jnp.dot(cells, kernels[n, s], preferred_element_type=F32))
             outgoing[n] = jnp.concatenate(parts, axis=0).astype(BF16)
+        if group == 0:
+            pl.semaphore_wait(barrier, expected)
+            start_halo(halo_copies(*halo))
         for n in members:
             if n < 15:
                 sends[n].start()
@@ -244,7 +243,7 @@
 def network_body(ext, cols_in, landed, target, land, rows_to, rate, couple, bias_out,
                  w_in, b_in, w_mid, b_mid, w_out,
                  new_state, dm, base, going, grads,
-                 remapped, other_cot, first_w, first_back, mid_turned, mid_half, out_half, w_out_turned, mid_bias, g_first, g_mid, g_out, g_bias, *kept):
+                 remapped, other_cot, first_w, first_back, mid_turned, mid_half, out_half, w_out_turned, wide_out, mid_bias, g_first, g_mid, g_out, g_bias, *kept):
     c, i, j = here()
     lane = lanes()
     peers = [entry(n, i, j) for n in range(ENTRIES)]
@@ -275,6 +274,8 @@
     tall = jnp.concatenate([w_out[...].astype(F32), jnp.zeros((TILE - 4, HID), F32)], axis=0)
     w_out_turned[...] = tall[:16].astype(BF16)
     out_half[...] = (0.5 * tall.T)[:, :16].astype(BF16)
+    for f in range(4):
+        wide_out[f] = jnp.broadcast_to(0.5 * tall[f:f + 1], (WIDE, HID)).T
     mid_bias[...] = jnp.broadcast_to(0.5 * b_mid[...], (TILE, HID)).T
     ones = (lax.broadcasted_iota(jnp.int32, (16, WIDE), 0) < 3).astype(BF16)
     for p in range(CHUNK * TILE // WIDE):
@@ -350,7 +351,11 @@
             g_bias[...] += cot.astype(F32)[:CH]
         flux_cot = jnp.concatenate(cots, axis=1)
         cot_ref[:, span] = flux_cot
-        pulled = jnp.dot(out_half[...], flux_cot, preferred_element_type=F32)
+        if part in SPREAD:
+            exact = flux_cot.astype(F32)
+            pulled = sum(wide_out[f] * exact[f:f + 1] for f in range(4))
+        else:
+            pulled = jnp.dot(out_half[...], flux_cot, preferred_element_type=F32)
         yield
         second_cot = (pulled * slope_two[:, span]).astype(BF16)
         two_ref[:, span] = second_cot
@@ -371,7 +376,6 @@
         g_first[...] += lax.dot_general(features_ref[...], one_ref[...], NT, preferred_element_type=F32)
 
     def play(*chains):
-        chains = list(chains)
         while chains:
             chains = [chain for chain in chains if next(chain, chain) is not chain]
 
@@ -383,7 +387,8 @@
     def both(back_at, back, front_at, front):
         chains = []
         for p in range(PARTS):
-            chains.append(forward(front_at, p, *front))
+            if front is not None:
+                chains.append(forward(front_at, p, *front))
             chains.append(backward(back_at, p, *back))
         play(*chains)
         gradients(*back)
@@ -391,10 +396,12 @@
     def step(pair, carry):
         at = pair * (2 * CHUNK)
         both(at, even, at + CHUNK, odd)
-        both(at + CHUNK, odd, jnp.minimum(at + 2 * CHUNK, TILE - CHUNK), even)
+        both(at + CHUNK, odd, at + 2 * CHUNK, even)
         return carry
 
-    lax.fori_loop(0, TILE // (2 * CHUNK), step, 0)
+    lax.fori_loop(0, TILE // (2 * CHUNK) - 1, step, 0)
+    both(TILE - 2 * CHUNK, even, TILE - CHUNK, odd)
+    both(TILE - CHUNK, odd, 0, None)
     zero = jnp.zeros((CH, TILE), F32)
     dm[0] = zero
     dm[TILE + 1] = zero
@@ -403,18 +410,19 @@
         going[n] = jnp.concatenate(
             [other_cot[rows_to[s, tile]] for s in range(SLOTS)], axis=0
         ).astype(BF16)
-    grads[0:256] = g_mid[:HID, :TILE]
-    grads[256:512] = g_mid[:HID, TILE:]
+    def pack(at, values):
+        grads[at:at + values.shape[0]] = values.astype(BF16)
+
     for side in range(2):
         columns = slice(side * TILE, (side + 1) * TILE)
-        at = 512 + side * 16
-        grads[at:at + 8] = jnp.where(flip, g_first[8:16, columns], g_first[0:8, columns])
-        grads[at + 8:at + 16] = jnp.where(flip, g_first[0:8, columns], g_first[8:16, columns])
-        grads[544 + side * 8:552 + side * 8] = g_first[16:24, columns]
-        grads[560 + side * 8:568 + side * 8] = g_mid[HID:HID + 8, columns]
-        grads[576 + side * 8:584 + side * 8] = g_out[:CH, columns]
-    grads[592:600] = g_bias[...]
-    grads[600:640] = jnp.zeros((40, TILE), F32)
+        pack(side * HID, g_mid[:HID, columns])
+        own, other, extra = g_first[0:8, columns], g_first[8:16, columns], g_first[16:32, columns]
+        pack(512 + side * 16, jnp.concatenate([jnp.where(flip, other, own), jnp.where(flip, own, other)], axis=0))
+        pack(544 + side * 16, extra)
+        pack(576 + side * 16, g_mid[HID:HID + 16, columns])
+        pack(608 + side * 16, g_out[:, columns])
+    pack(640, jnp.concatenate([g_bias[...], jnp.zeros((CH, TILE), F32)], axis=0))
+    pack(656, jnp.zeros((16 * PIECE - 656, TILE), F32))
 
 
 def return_body(going, dm_in, base, grads, weights, source, count, rate,
@@ -424,7 +432,6 @@
     c, i, j = here()
     lane = lanes()
     barrier = pltpu.get_barrier_semaphore()
-    expected = greet(barrier, c, i, j) + 22
     me = c * 4 + i
     across = [(j + d) % 16 for d in range(1, 16)]
     along = [((me + d) % 8 // 4, (me + d) % 4) for d in range(1, 8)]
@@ -432,14 +439,13 @@
         signal_to(barrier, (c, i, col))
     for other in along:
         signal_to(barrier, (*other, j))
+    expected = greet(barrier, c, i, j) + 22
     peers = [entry(n, i, j) for n in range(ENTRIES)]
     loads = []
     for n, (_, row, col, _) in enumerate(peers):
         load = pltpu.make_async_copy(weights.at[row * 16 + col], kernels.at[n], load_sem.at[n])
         load.start()
         loads.append(load)
-    dm[...] = dm_in[...]
-    edge_columns(dm, cols_out)
     pl.semaphore_wait(barrier, expected)
     halo = (c, i, j, dm, cols_out, cols_in, rows_in, hsend_sem, hrecv_sem)
     phase1 = [
@@ -447,7 +453,6 @@
     ]
     for copy in phase1:
         copy.start()
-    start_halo(halo_copies(*halo))
     sends = []
     for n, (valid, row, col, place) in enumerate(peers):
         copy = remote(going.at[n], back_in.at[place], send_sem.at[n], recv_sem.at[place], (1 - c, row, col))
@@ -456,6 +461,9 @@
             copy.start()
         else:
             pl.when(valid == 1)(copy.start)
+    dm[...] = dm_in[...]
+    edge_columns(dm, cols_out)
+    start_halo(halo_copies(*halo))
 
     for n, (_, row, col, _) in enumerate(peers):
         tile = row * 16 + col
@@ -471,12 +479,13 @@
 
     for copy in phase1:
         copy.wait_recv()
-    partial = grads[j]
+    partial = grads[j].astype(F32)
     for d in range(15):
-        partial = partial + first_in[d]
-    mid_sum[...] = partial
+        partial = partial + first_in[d].astype(F32)
+    mid_sum[...] = partial.astype(BF16)
+    second_in[me] = partial.astype(BF16)
     phase2 = [
-        remote(mid_sum, second_in.at[d], s2.at[d], r2.at[d], (*other, j)) for d, other in enumerate(along)
+        remote(mid_sum, second_in.at[me], s2.at[d], r2.at[d], (*other, j)) for d, other in enumerate(along)
     ]
     for copy in phase2:
         copy.start()
@@ -495,13 +504,13 @@
 
     lax.fori_loop(0, TILE // 8, step, 0)
 
-    for copy in phase2:
-        copy.wait_recv()
-    partial = mid_sum[...]
     for d in range(7):
-        partial = partial + second_in[d]
-    total[...] = partial
-    whole[j] = partial
+        remote(mid_sum, second_in.at[(me + 7 - d) % 8], s2.at[d], r2.at[d], (*along[d], j)).wait_recv()
+    partial = second_in[0].astype(F32)
+    for d in range(1, 8):
+        partial = partial + second_in[d].astype(F32)
+    total[...] = partial.astype(BF16)
+    whole[j] = partial.astype(BF16)
     phase3 = [
         remote(total, whole.at[j], s3.at[d], r3.at[d], (c, i, col)) for d, col in enumerate(across)
     ]
@@ -550,15 +559,15 @@
 def finish_body(adjoint_in, whole, adjoint, o_w_in, o_b_in, o_w_mid, o_b_mid, o_w_out, o_b_out, sem):
     copy = pltpu.make_async_copy(adjoint_in, adjoint, sem)
     copy.start()
-    flat = whole[...] * (1.0 / 1048576.0)
+    flat = whole[...].astype(F32) * (1.0 / 1048576.0)
     for side in range(2):
         columns = slice(side * TILE, (side + 1) * TILE)
         o_w_mid[:, columns] = flat[side * HID:(side + 1) * HID]
         o_w_in[:, columns] = flat[512 + side * 16:528 + side * 16]
-        o_b_in[:, columns] = flat[544 + side * 8:545 + side * 8]
-        o_b_mid[:, columns] = flat[560 + side * 8:561 + side * 8]
-        o_w_out[:, columns] = flat[576 + side * 8:580 + side * 8]
-    sums = jnp.broadcast_to(jnp.sum(flat[592:600], axis=1, keepdims=True), (CH, TILE))
+        o_b_in[:, columns] = flat[544 + side * 16:545 + side * 16]
+        o_b_mid[:, columns] = flat[576 + side * 16:577 + side * 16]
+        o_w_out[:, columns] = flat[608 + side * 16:612 + side * 16]
+    sums = jnp.broadcast_to(jnp.sum(flat[640:648], axis=1, keepdims=True), (CH, TILE))
     sub = lax.broadcasted_iota(jnp.int32, (CH, TILE), 0)
     picked = jnp.sum(jnp.where(sub == lanes(), sums, 0.0), axis=0, keepdims=True)
     o_b_out[...] = picked[:, :4]
@@ -583,7 +592,7 @@
             arr((TILE + 2, CH, TILE)),
             arr((TILE, CH, TILE)),
             arr((ENTRIES, SLOTS * CH, TILE), BF16),
-            arr((16 * PIECE, TILE)),
+            arr((16 * PIECE, TILE), BF16),
         ),
         in_specs=[VM] * 5 + [SM] * 4 + [VM] * 5,
         out_specs=(VM,) * 5,
@@ -596,6 +605,7 @@
             pltpu.VMEM((HID, HID), BF16),
             pltpu.VMEM((HID, 16), BF16),
             pltpu.VMEM((16, HID), BF16),
+            pltpu.VMEM((4, HID, WIDE), F32),
             pltpu.VMEM((HID, TILE), F32),
             pltpu.VMEM((32, HID), F32),
             pltpu.VMEM((HID + 16, HID), F32),
@@ -655,7 +665,7 @@
 
     adjoint, whole = pl.pallas_call(
         return_body,
-        out_shape=(arr((CH * TILE, TILE)), arr((16, PIECE, TILE))),
+        out_shape=(arr((CH * TILE, TILE)), arr((16, PIECE, TILE), BF16)),
         in_specs=[VM] * 4 + [HB] + [SM] * 3,
         out_specs=(VM, VM),
         scratch_shapes=[
@@ -667,10 +677,10 @@
             pltpu.VMEM((3, CH, TILE), F32),
             pltpu.VMEM((ENTRIES * SLOTS * CH, TILE), F32),
             pltpu.VMEM((TILE, TILE), F32),
-            pltpu.VMEM((15, PIECE, TILE), F32),
-            pltpu.VMEM((PIECE, TILE), F32),
-            pltpu.VMEM((7, PIECE, TILE), F32),
-            pltpu.VMEM((PIECE, TILE), F32),
+            pltpu.VMEM((15, PIECE, TILE), BF16),
+            pltpu.VMEM((PIECE, TILE), BF16),
+            pltpu.VMEM((8, PIECE, TILE), BF16),
+            pltpu.VMEM((PIECE, TILE), BF16),
             DMA((ENTRIES,)), DMA((ENTRIES,)), DMA((ENTRIES,)), DMA((5,)), DMA((5,)),
             DMA((15,)), DMA((15,)), DMA((7,)), DMA((7,)), DMA((15,)), DMA((15,)),
         ],

time: 69 us -> 66.5 us (0.964)
  Pallas kernels: 67.7 us -> 65.5 us
    pallas_call x1, Pallas kernels: 24 us -> 23.1 us  [shards(): pl.pallas_call(return_body, out_shape=(arr((CH * TILE, TILE)), arr((16, P...]
    pallas_call x1, Pallas kernels: 15.5 us -> 14.8 us  [shards(): pl.pallas_call(send_body, out_shape=(arr((TILE + 2, CH, TILE)), arr((2, C...]
where the time goes in v3:
time: 66.5 us; the launch traced here: 66.4 us
  Pallas kernels  65.5 us (98%)
  between operations  0.85 us (1%)
    pallas_call x1, Pallas kernels, network_call(): pl.pallas_call(network_body, out_shape=(arr((CH * TILE, TILE)), arr((TILE...  26.1 us
    pallas_call x1, Pallas kernels, shards(): pl.pallas_call(return_body, out_shape=(arr((CH * TILE, TILE)), arr((16, P...  23.1 us
    pallas_call x1, Pallas kernels, shards(): pl.pallas_call(send_body, out_shape=(arr((TILE + 2, CH, TILE)), arr((2, C...  14.8 us
    pallas_call x1, Pallas kernels, shards(): pl.pallas_call(finish_body, out_shape=(arr((CH * TILE, TILE)), arr((16, H...  1.53 us

profile of v3, /device:TPU:0, one launch (start us, length us, event | category | flops | bytes accessed | tf_op | source)
XLA Modules:
  0.0 66.4 jit_solution(4922195658405305014)
XLA Ops:
  0.6 0.0 copy-start.6
  0.6 0.0 copy-start.9
  0.7 0.0 copy-start.7
  0.7 0.0 copy-start.4
  0.7 0.0 copy-start.12
  0.7 0.0 copy-start.8
  0.7 0.0 copy-start.11
  0.7 0.0 copy-start.1
  0.7 0.0 copy-start.10
  0.7 0.0 copy-start.3
  0.7 0.0 copy-start.5
  0.7 0.0 copy-start.2
  0.8 0.0 copy-start
  0.8 14.8 %remap_send.1 = (f32[130,8,128]{2,1,0:T(8,128)S(1)}, f32[2,8,128]{2,1,0:T(8,128)S(1)}, bf16[20,32,128]{2,1,0:T(8,128)(2,1)S(1)}) custom-call(f32[1024,128]{1,0:T(8,128)} %bitcast.40, bf16[64,4,128,128]{3,2,1,0:T(8,128)(2,1)} %bitcast.38, s32[4,64]{1,0:T(4,128)} %bitcast.28, s32[1,64]{1,0:T(1,128)} %bitcast.33), custom_call_target="tpu_custom_call" | custom-call | tf_op jit(solution)/shard_map/remap_send/pallas_call | solution.py:640
  15.6 0.0 copy-done.6
  15.6 0.0 copy-done.7
  15.6 0.0 copy-done.12
  15.6 0.0 copy-done.8
  15.6 0.0 copy-done.11
  15.6 0.0 copy-done.1
  15.6 0.0 copy-done.10
  15.7 26.1 %network.1 = (f32[1024,128]{1,0:T(8,128)}, f32[130,8,128]{2,1,0:T(8,128)S(1)}, f32[128,8,128]{2,1,0:T(8,128)S(1)}, bf16[20,32,128]{2,1,0:T(8,128)(2,1)S(1)}, bf16[768,128]{1,0:T(8,128)(2,1)S(1)}) custom-call(f32[130,8,128]{2,1,0:T(8,128)S(1)} %get-tuple-element.25.ext, f32[2,8,128]{2,1,0:T(8,128)S(1)} %get-tuple-element.26.cols_in, ...), custom_call_target="tpu_custom_call" | custom-call | tf_op jit(solution)/shard_map/network/pallas_call | solution.py:588
  41.8 23.1 %remap_return.1 = (f32[1024,128]{1,0:T(8,128)S(1)}, bf16[16,48,128]{2,1,0:T(8,128)(2,1)S(1)}) custom-call(bf16[20,32,128]{2,1,0:T(8,128)(2,1)S(1)} %get-tuple-element.29.going, f32[130,8,128]{2,1,0:T(8,128)S(1)} %get-tuple-element.30.dm_in, f32[128,8,128]{2,1,0:T(8,128)S(1)} %get-tuple-element.31.base, bf16[16,48,128]{2,1,0:T(8,128)(2,1)S(1)} %bitcast.26, ...), custom_call_target="tpu_custom_call" | custom-call | tf_op jit(solution)/shard_map/remap_return/pallas_call | solution.py:666
  64.9 1.5 %finish.1 = (f32[1024,128]{1,0:T(8,128)}, f32[16,256]{1,0:T(8,128)}, f32[1,256]{1,0:T(1,128)}, f32[256,256]{1,0:T(8,128)}, f32[1,256]{1,0:T(1,128)}, /*index=5*/f32[4,256]{1,0:T(4,128)}, f32[1,4]{1,0:T(1,128)}) custom-call(f32[1024,128]{1,0:T(8,128)S(1)} %get-tuple-element.33.adjoint_in, bf16[768,128]{1,0:T(8,128)(2,1)S(1)} %bitcast.25), custom_call_target="tpu_custom_call" | custom-call | tf_op jit(solution)/shard_map/finish/pallas_call | solution.py:694
  (6 shorter events, 0.0 us)
Async XLA Ops:
  0.6 14.9 %copy-start.6 = (f32[2,8]{1,0:T(2,128)S(1)}, f32[2,8]{1,0:T(2,128)}, u32[]{:S(2)}) copy-start(f32[2,8]{1,0:T(2,128)} %rate.3) | copy-start | bytes 196
  0.6 41.1 %copy-start.9 = (s32[1,1,1,64]{3,2,1,0:T(1,128)S(1)}, s32[1,1,1,64]{3,2,1,0:T(1,128)}, u32[]{:S(2)}) copy-start(s32[1,1,1,64]{3,2,1,0:T(1,128)} %param.29) | copy-start | bytes 772
  0.7 14.9 %copy-start.7 = (s32[1,1,1,64,4]{3,4,2,1,0:T(4,128)S(1)}, s32[1,1,1,64,4]{3,4,2,1,0:T(4,128)}, u32[]{:S(2)}) copy-start(s32[1,1,1,64,4]{3,4,2,1,0:T(4,128)} %param.28) | copy-start | bytes 3076
  0.7 41.1 %copy-start.4 = (s32[1,1,1,64,4]{3,4,2,1,0:T(4,128)S(1)}, s32[1,1,1,64,4]{3,4,2,1,0:T(4,128)}, u32[]{:S(2)}) copy-start(s32[1,1,1,64,4]{3,4,2,1,0:T(4,128)} %param.27) | copy-start | bytes 3076
  0.7 14.9 %copy-start.12 = (f32[4]{0:T(128)S(1)}, f32[4]{0:T(128)}, u32[]{:S(2)}) copy-start(f32[4]{0:T(128)} %param.25) | copy-start | bytes 52
  0.7 14.9 %copy-start.8 = (bf16[256,4]{0,1:T(4,128)(2,1)S(1)}, bf16[256,4]{0,1:T(4,128)(2,1)}, u32[]{:S(2)}) copy-start(bf16[256,4]{0,1:T(4,128)(2,1)} %param.24) | copy-start | bytes 6148
  0.7 14.9 %copy-start.11 = (f32[256]{0:T(256)S(1)}, f32[256]{0:T(256)}, u32[]{:S(2)}) copy-start(f32[256]{0:T(256)} %param.23) | copy-start | bytes 3076
  0.7 14.9 %copy-start.1 = (bf16[256,256]{1,0:T(8,128)(2,1)S(1)}, bf16[256,256]{1,0:T(8,128)(2,1)}, u32[]{:S(2)}) copy-start(bf16[256,256]{1,0:T(8,128)(2,1)} %w_mid.1) | copy-start | bytes 393220
  0.7 14.9 %copy-start.10 = (f32[256]{0:T(256)S(1)}, f32[256]{0:T(256)}, u32[]{:S(2)}) copy-start(f32[256]{0:T(256)} %param.21) | copy-start | bytes 3076
  0.7 14.9 %copy-start.3 = (bf16[16,256]{1,0:T(8,128)(2,1)S(1)}, bf16[16,256]{1,0:T(8,128)(2,1)}, u32[]{:S(2)}) copy-start(bf16[16,256]{1,0:T(8,128)(2,1)} %w_in.1) | copy-start | bytes 24580
  0.7 14.9 %copy-start.5 = (f32[2,8,4]{1,2,0:T(4,128)S(1)}, f32[2,8,4]{1,2,0:T(4,128)}, u32[]{:S(2)}) copy-start(f32[2,8,4]{1,2,0:T(4,128)} %param.19) | copy-start | bytes 772
  0.7 14.9 %copy-start.2 = (s32[1,128,128]{2,1,0:T(8,128)S(1)}, s32[1,128,128]{2,1,0:T(8,128)}, u32[]{:S(2)}) copy-start(s32[1,128,128]{2,1,0:T(8,128)} %param.17) | copy-start | bytes 196612
  0.8 14.9 %copy-start = (f32[1,8,128,128]{3,2,1,0:T(8,128)S(1)}, f32[1,8,128,128]{3,2,1,0:T(8,128)}, u32[]{:S(2)}) copy-start(f32[1,8,128,128]{3,2,1,0:T(8,128)} %param.16) | copy-start | bytes 1572868

commit v4 on v3

--- a/solution.py
+++ b/solution.py
@@ -274,8 +274,8 @@
     tall = jnp.concatenate([w_out[...].astype(F32), jnp.zeros((TILE - 4, HID), F32)], axis=0)
     w_out_turned[...] = tall[:16].astype(BF16)
     out_half[...] = (0.5 * tall.T)[:, :16].astype(BF16)
-    for f in range(4):
-        wide_out[f] = jnp.broadcast_to(0.5 * tall[f:f + 1], (WIDE, HID)).T
+    pick = lax.broadcasted_iota(jnp.int32, (16, 4 * TILE), 0) == lax.broadcasted_iota(jnp.int32, (16, 4 * TILE), 1) // TILE
+    wide_out[...] = jnp.dot(out_half[...], pick.astype(BF16), preferred_element_type=F32)
     mid_bias[...] = jnp.broadcast_to(0.5 * b_mid[...], (TILE, HID)).T
     ones = (lax.broadcasted_iota(jnp.int32, (16, WIDE), 0) < 3).astype(BF16)
     for p in range(CHUNK * TILE // WIDE):
@@ -353,7 +353,13 @@
         cot_ref[:, span] = flux_cot
         if part in SPREAD:
             exact = flux_cot.astype(F32)
-            pulled = sum(wide_out[f] * exact[f:f + 1] for f in range(4))
+            pulled = jnp.concatenate(
+                [
+                    sum(wide_out[:, f * TILE:(f + 1) * TILE] * exact[f:f + 1, k * TILE:(k + 1) * TILE] for f in range(4))
+                    for k in range(WIDE // TILE)
+                ],
+                axis=1,
+            )
         else:
             pulled = jnp.dot(out_half[...], flux_cot, preferred_element_type=F32)
         yield
@@ -425,11 +431,17 @@
     pack(656, jnp.zeros((16 * PIECE - 656, TILE), F32))
 
 
-def return_body(going, dm_in, base, grads, weights, source, count, rate,
+def return_body(going, dm_in, base, grads, weights, source_in, count_in, rate_in,
                 adjoint, whole,
-                dm, kernels, back_in, cols_out, cols_in, rows_in, spread, anchor, first_in, mid_sum, second_in, total,
-                load_sem, send_sem, recv_sem, hsend_sem, hrecv_sem, s1, r1, s2, r2, s3, r3):
+                source, count, rate, dm, kernels, back_in, cols_out, cols_in, rows_in, spread, anchor, first_in, mid_sum, second_in, total,
+                load_sem, send_sem, recv_sem, hsend_sem, hrecv_sem, s1, r1, s2, r2, s3, r3, in_sem):
     c, i, j = here()
+    tables = [
+        pltpu.make_async_copy(given, held, in_sem.at[k])
+        for k, (given, held) in enumerate(((source_in, source), (count_in, count), (rate_in, rate)))
+    ]
+    for load in tables:
+        load.start()
     lane = lanes()
     barrier = pltpu.get_barrier_semaphore()
     me = c * 4 + i
@@ -465,6 +477,8 @@
     edge_columns(dm, cols_out)
     start_halo(halo_copies(*halo))
 
+    for load in tables:
+        load.wait()
     for n, (_, row, col, _) in enumerate(peers):
         tile = row * 16 + col
         live = count[0, tile]
@@ -556,9 +570,12 @@
         copy.wait_send()
 
 
-def finish_body(adjoint_in, whole, adjoint, o_w_in, o_b_in, o_w_mid, o_b_mid, o_w_out, o_b_out, sem):
-    copy = pltpu.make_async_copy(adjoint_in, adjoint, sem)
-    copy.start()
+def finish_body(adjoint_in, state_in, whole, adjoint, new_state, o_w_in, o_b_in, o_w_mid, o_b_mid, o_w_out, o_b_out, sem):
+    copies = [
+        pltpu.make_async_copy(adjoint_in, adjoint, sem.at[0]), pltpu.make_async_copy(state_in, new_state, sem.at[1])
+    ]
+    for copy in copies:
+        copy.start()
     flat = whole[...].astype(F32) * (1.0 / 1048576.0)
     for side in range(2):
         columns = slice(side * TILE, (side + 1) * TILE)
@@ -571,7 +588,8 @@
     sub = lax.broadcasted_iota(jnp.int32, (CH, TILE), 0)
     picked = jnp.sum(jnp.where(sub == lanes(), sums, 0.0), axis=0, keepdims=True)
     o_b_out[...] = picked[:, :4]
-    copy.wait()
+    for copy in copies:
+        copy.wait()
 
 
 VM = pl.BlockSpec(memory_space=pltpu.VMEM)
@@ -605,7 +623,7 @@
             pltpu.VMEM((HID, HID), BF16),
             pltpu.VMEM((HID, 16), BF16),
             pltpu.VMEM((16, HID), BF16),
-            pltpu.VMEM((4, HID, WIDE), F32),
+            pltpu.VMEM((HID, 4 * TILE), F32),
             pltpu.VMEM((HID, TILE), F32),
             pltpu.VMEM((32, HID), F32),
             pltpu.VMEM((HID + 16, HID), F32),
@@ -666,9 +684,12 @@
     adjoint, whole = pl.pallas_call(
         return_body,
         out_shape=(arr((CH * TILE, TILE)), arr((16, PIECE, TILE), BF16)),
-        in_specs=[VM] * 4 + [HB] + [SM] * 3,
+        in_specs=[VM] * 4 + [HB] * 4,
         out_specs=(VM, VM),
         scratch_shapes=[
+            pltpu.SMEM((SLOTS, 64), jnp.int32),
+            pltpu.SMEM((1, 64), jnp.int32),
+            pltpu.SMEM((2, CH), F32),
             pltpu.VMEM((TILE + 2, CH, TILE), F32),
             pltpu.VMEM((ENTRIES, SLOTS, TILE, TILE), BF16),
             pltpu.VMEM((ENTRIES, SLOTS * CH, TILE), BF16),
@@ -682,27 +703,27 @@
             pltpu.VMEM((8, PIECE, TILE), BF16),
             pltpu.VMEM((PIECE, TILE), BF16),
             DMA((ENTRIES,)), DMA((ENTRIES,)), DMA((ENTRIES,)), DMA((5,)), DMA((5,)),
-            DMA((15,)), DMA((15,)), DMA((7,)), DMA((7,)), DMA((15,)), DMA((15,)),
+            DMA((15,)), DMA((15,)), DMA((7,)), DMA((7,)), DMA((15,)), DMA((15,)), DMA((3,)),
         ],
         compiler_params=pltpu.CompilerParams(
             collective_id=1, has_side_effects=True, vmem_limit_bytes=32 << 20
         ),
         name="remap_return",
     )(
-        going, dm, base, grads.reshape(16, PIECE, TILE), pltpu.with_memory_space_constraint(weights, pltpu.HBM), source, count, diffusivity
+        going, dm, base, grads.reshape(16, PIECE, TILE), *(pltpu.with_memory_space_constraint(a, pltpu.HBM) for a in (weights, source, count, diffusivity))
     )
-    adjoint, g_w_in, g_b_in, g_w_mid, g_b_mid, g_w_out, g_b_out = pl.pallas_call(
+    adjoint, new_state, g_w_in, g_b_in, g_w_mid, g_b_mid, g_w_out, g_b_out = pl.pallas_call(
         finish_body,
         out_shape=(
-            arr((CH * TILE, TILE)), arr((16, HID)), arr((1, HID)), arr((HID, HID)), arr((1, HID)),
+            arr((CH * TILE, TILE)), arr((CH * TILE, TILE)), arr((16, HID)), arr((1, HID)), arr((HID, HID)), arr((1, HID)),
             arr((4, HID)), arr((1, 4)),
         ),
-        in_specs=[VM, VM],
-        out_specs=(HB,) + (VM,) * 6,
-        scratch_shapes=[DMA],
+        in_specs=[VM, VM, VM],
+        out_specs=(HB, HB) + (VM,) * 6,
+        scratch_shapes=[DMA((2,))],
         compiler_params=pltpu.CompilerParams(vmem_limit_bytes=8 << 20),
         name="finish",
-    )(adjoint, whole.reshape(16 * PIECE, TILE))
+    )(adjoint, new_state, whole.reshape(16 * PIECE, TILE))
     return (
         new_state.reshape(1, CH, TILE, TILE),
         adjoint.reshape(1, CH, TILE, TILE),

time: 66.5 us -> 66 us (level)
  no operation moved by 1% of the time
where the time goes in v4:
time: 66 us; the launch traced here: 65.9 us
  Pallas kernels  65 us (98%)
  between operations  0.83 us (1%)
    pallas_call x1, Pallas kernels, network_call(): pl.pallas_call(network_body, out_shape=(arr((CH * TILE, TILE)), arr((TILE...  25.9 us
    pallas_call x1, Pallas kernels, shards(): pl.pallas_call(return_body, out_shape=(arr((CH * TILE, TILE)), arr((16, P...  22.6 us
    pallas_call x1, Pallas kernels, shards(): pl.pallas_call(send_body, out_shape=(arr((TILE + 2, CH, TILE)), arr((2, C...  14.8 us
    pallas_call x1, Pallas kernels, shards(): pl.pallas_call(finish_body, out_shape=(arr((CH * TILE, TILE)), arr((CH *...  1.71 us

profile of v4, /device:TPU:0, one launch (start us, length us, event | category | flops | bytes accessed | tf_op | source)
XLA Modules:
  0.0 65.9 jit_solution(8178300444753807827)
XLA Ops:
  0.6 0.0 copy-start.5
  0.6 0.0 copy-start.6
  0.7 0.0 copy-start.10
  0.7 0.0 copy-start.7
  0.7 0.0 copy-start.9
  0.7 0.0 copy-start.1
  0.7 0.0 copy-start.8
  0.7 0.0 copy-start.3
  0.7 0.0 copy-start.4
  0.7 14.8 %remap_send.1 = (f32[130,8,128]{2,1,0:T(8,128)S(1)}, f32[2,8,128]{2,1,0:T(8,128)S(1)}, bf16[20,32,128]{2,1,0:T(8,128)(2,1)S(1)}) custom-call(f32[1024,128]{1,0:T(8,128)} %bitcast.36, bf16[64,4,128,128]{3,2,1,0:T(8,128)(2,1)} %bitcast.34, s32[4,64]{1,0:T(4,128)} %bitcast.37, s32[1,64]{1,0:T(1,128)} %bitcast.39), custom_call_target="tpu_custom_call" | custom-call | tf_op jit(solution)/shard_map/remap_send/pallas_call | solution.py:658
  15.5 0.0 copy-done.5
  15.6 0.0 copy-done.6
  15.6 0.0 copy-done.10
  15.6 0.0 copy-done.7
  15.6 0.0 copy-done.9
  15.6 0.0 copy-done.1
  15.6 0.0 copy-done.8
  15.6 0.0 copy-done.3
  15.6 0.0 copy-done.4
  15.6 0.0 copy-done.2
  15.6 0.0 copy-done
  15.7 25.9 %network.1 = (f32[1024,128]{1,0:T(8,128)S(1)}, f32[130,8,128]{2,1,0:T(8,128)S(1)}, f32[128,8,128]{2,1,0:T(8,128)S(1)}, bf16[20,32,128]{2,1,0:T(8,128)(2,1)S(1)}, bf16[768,128]{1,0:T(8,128)(2,1)S(1)}) custom-call(f32[130,8,128]{2,1,0:T(8,128)S(1)} %get-tuple-element.26.ext, f32[2,8,128]{2,1,0:T(8,128)S(1)} %get-tuple-element.27.cols_in, ...), custom_call_target="tpu_custom_call" | custom-call | tf_op jit(solution)/shard_map/network/pallas_call | solution.py:606
  41.6 22.6 %remap_return.1 = (f32[1024,128]{1,0:T(8,128)S(1)}, bf16[16,48,128]{2,1,0:T(8,128)(2,1)S(1)}) custom-call(bf16[20,32,128]{2,1,0:T(8,128)(2,1)S(1)} %get-tuple-element.29.going, f32[130,8,128]{2,1,0:T(8,128)S(1)} %get-tuple-element.30.dm_in, f32[128,8,128]{2,1,0:T(8,128)S(1)} %get-tuple-element.31.base, bf16[16,48,128]{2,1,0:T(8,128)(2,1)S(1)} %bitcast.26, ...), custom_call_target="tpu_custom_call" | custom-call | tf_op jit(solution)/shard_map/remap_return/pallas_call | solution.py:684
  64.2 1.7 %finish.1 = (f32[1024,128]{1,0:T(8,128)}, f32[1024,128]{1,0:T(8,128)}, f32[16,256]{1,0:T(8,128)}, f32[1,256]{1,0:T(1,128)}, f32[256,256]{1,0:T(8,128)}, /*index=...) custom-call(f32[1024,128]{1,0:T(8,128)S(1)} %get-tuple-element.33.adjoint_in, ...), custom_call_target="tpu_custom_call" | custom-call | tf_op jit(solution)/shard_map/finish/pallas_call | solution.py:715
  (2 shorter events, 0.0 us)
Async XLA Ops:
  0.6 14.9 %copy-start.5 = (f32[2,8]{1,0:T(2,128)S(1)}, f32[2,8]{1,0:T(2,128)}, u32[]{:S(2)}) copy-start(f32[2,8]{1,0:T(2,128)} %rate_in.1) | copy-start | bytes 196
  0.6 14.9 %copy-start.6 = (s32[1,1,1,64,4]{3,4,2,1,0:T(4,128)S(1)}, s32[1,1,1,64,4]{3,4,2,1,0:T(4,128)}, u32[]{:S(2)}) copy-start(s32[1,1,1,64,4]{3,4,2,1,0:T(4,128)} %param.28) | copy-start | bytes 3076
  0.7 14.9 %copy-start.10 = (f32[4]{0:T(128)S(1)}, f32[4]{0:T(128)}, u32[]{:S(2)}) copy-start(f32[4]{0:T(128)} %param.25) | copy-start | bytes 52
  0.7 14.9 %copy-start.7 = (bf16[256,4]{0,1:T(4,128)(2,1)S(1)}, bf16[256,4]{0,1:T(4,128)(2,1)}, u32[]{:S(2)}) copy-start(bf16[256,4]{0,1:T(4,128)(2,1)} %param.24) | copy-start | bytes 6148
  0.7 14.9 %copy-start.9 = (f32[256]{0:T(256)S(1)}, f32[256]{0:T(256)}, u32[]{:S(2)}) copy-start(f32[256]{0:T(256)} %param.23) | copy-start | bytes 3076
  0.7 14.9 %copy-start.1 = (bf16[256,256]{1,0:T(8,128)(2,1)S(1)}, bf16[256,256]{1,0:T(8,128)(2,1)}, u32[]{:S(2)}) copy-start(bf16[256,256]{1,0:T(8,128)(2,1)} %w_mid.1) | copy-start | bytes 393220
  0.7 14.9 %copy-start.8 = (f32[256]{0:T(256)S(1)}, f32[256]{0:T(256)}, u32[]{:S(2)}) copy-start(f32[256]{0:T(256)} %param.21) | copy-start | bytes 3076
  0.7 14.9 %copy-start.3 = (bf16[16,256]{1,0:T(8,128)(2,1)S(1)}, bf16[16,256]{1,0:T(8,128)(2,1)}, u32[]{:S(2)}) copy-start(bf16[16,256]{1,0:T(8,128)(2,1)} %w_in.1) | copy-start | bytes 24580
  0.7 14.9 %copy-start.4 = (f32[2,8,4]{1,2,0:T(4,128)S(1)}, f32[2,8,4]{1,2,0:T(4,128)}, u32[]{:S(2)}) copy-start(f32[2,8,4]{1,2,0:T(4,128)} %param.19) | copy-start | bytes 772
  0.7 14.9 %copy-start.2 = (s32[1,128,128]{2,1,0:T(8,128)S(1)}, s32[1,128,128]{2,1,0:T(8,128)}, u32[]{:S(2)}) copy-start(s32[1,128,128]{2,1,0:T(8,128)} %param.17) | copy-start | bytes 196612
  0.7 14.9 %copy-start = (f32[1,8,128,128]{3,2,1,0:T(8,128)S(1)}, f32[1,8,128,128]{3,2,1,0:T(8,128)}, u32[]{:S(2)}) copy-start(f32[1,8,128,128]{3,2,1,0:T(8,128)} %param.16) | copy-start | bytes 1572868

commit v5 on v4

--- a/solution.py
+++ b/solution.py
@@ -377,11 +377,15 @@
             other_cot[first_row + k] = piece[CH:]
 
     def gradients(features_ref, hidden_ref, slope_one, slope_two, second_ref, raw_ref, one_ref, two_ref, cot_ref):
+        g_out[...] += lax.dot_general(cot_ref[...], second_ref[...], NT, preferred_element_type=F32)
+        yield
         g_mid[...] += lax.dot_general(hidden_ref[...], two_ref[...], NT, preferred_element_type=F32)
-        g_out[...] += lax.dot_general(cot_ref[...], second_ref[...], NT, preferred_element_type=F32)
+        yield
         g_first[...] += lax.dot_general(features_ref[...], one_ref[...], NT, preferred_element_type=F32)
+        yield
 
     def play(*chains):
+        chains = list(chains)
         while chains:
             chains = [chain for chain in chains if next(chain, chain) is not chain]
 
@@ -393,11 +397,10 @@
     def both(back_at, back, front_at, front):
         chains = []
         for p in range(PARTS):
+            chains.append(backward(back_at, p, *back))
             if front is not None:
                 chains.append(forward(front_at, p, *front))
-            chains.append(backward(back_at, p, *back))
-        play(*chains)
-        gradients(*back)
+        play(*chains, gradients(*back))
 
     def step(pair, carry):
         at = pair * (2 * CHUNK)

time: 66 us -> 66.7 us (1.011)
  Pallas kernels: 65 us -> 65.7 us
    pallas_call x1, Pallas kernels: 25.9 us -> 26.6 us  [network_call(): pl.pallas_call(network_body, out_shape=(arr((CH * TILE, TILE)), arr((TILE...]
where the time goes in v5:
time: 66.7 us; the launch traced here: 66.6 us
  Pallas kernels  65.7 us (99%)
  between operations  0.83 us (1%)
    pallas_call x1, Pallas kernels, network_call(): pl.pallas_call(network_body, out_shape=(arr((CH * TILE, TILE)), arr((TILE...  26.6 us
    pallas_call x1, Pallas kernels, shards(): pl.pallas_call(return_body, out_shape=(arr((CH * TILE, TILE)), arr((16, P...  22.6 us
    pallas_call x1, Pallas kernels, shards(): pl.pallas_call(send_body, out_shape=(arr((TILE + 2, CH, TILE)), arr((2, C...  14.8 us
    pallas_call x1, Pallas kernels, shards(): pl.pallas_call(finish_body, out_shape=(arr((CH * TILE, TILE)), arr((CH *...  1.71 us

profile of v5, /device:TPU:0, one launch (start us, length us, event | category | flops | bytes accessed | tf_op | source)
XLA Modules:
  0.0 66.6 jit_solution(9468752509182556455)
XLA Ops:
  0.6 0.0 copy-start.5
  0.6 0.0 copy-start.6
  0.7 0.0 copy-start.10
  0.7 0.0 copy-start.7
  0.7 0.0 copy-start.9
  0.7 0.0 copy-start.1
  0.7 0.0 copy-start.8
  0.7 0.0 copy-start.3
  0.7 0.0 copy-start.4
  0.7 0.0 copy-start.2
  0.7 0.0 copy-start
  0.7 14.8 %remap_send.1 = (f32[130,8,128]{2,1,0:T(8,128)S(1)}, f32[2,8,128]{2,1,0:T(8,128)S(1)}, bf16[20,32,128]{2,1,0:T(8,128)(2,1)S(1)}) custom-call(f32[1024,128]{1,0:T(8,128)} %bitcast.36, bf16[64,4,128,128]{3,2,1,0:T(8,128)(2,1)} %bitcast.34, s32[4,64]{1,0:T(4,128)} %bitcast.37, s32[1,64]{1,0:T(1,128)} %bitcast.39), custom_call_target="tpu_custom_call" | custom-call | tf_op jit(solution)/shard_map/remap_send/pallas_call | solution.py:661
  15.5 0.0 copy-done.5
  15.6 0.0 copy-done.6
  15.6 0.0 copy-done.10
  15.6 0.0 copy-done.7
  15.6 0.0 copy-done.9
  15.6 0.0 copy-done.1
  15.6 0.0 copy-done.8
  15.6 0.0 copy-done.3
  15.6 0.0 copy-done.4
  15.7 26.6 %network.1 = (f32[1024,128]{1,0:T(8,128)S(1)}, f32[130,8,128]{2,1,0:T(8,128)S(1)}, f32[128,8,128]{2,1,0:T(8,128)S(1)}, bf16[20,32,128]{2,1,0:T(8,128)(2,1)S(1)}, bf16[768,128]{1,0:T(8,128)(2,1)S(1)}) custom-call(f32[130,8,128]{2,1,0:T(8,128)S(1)} %get-tuple-element.26.ext, f32[2,8,128]{2,1,0:T(8,128)S(1)} %get-tuple-element.27.cols_in, ...), custom_call_target="tpu_custom_call" | custom-call | tf_op jit(solution)/shard_map/network/pallas_call | solution.py:609
  42.2 22.6 %remap_return.1 = (f32[1024,128]{1,0:T(8,128)S(1)}, bf16[16,48,128]{2,1,0:T(8,128)(2,1)S(1)}) custom-call(bf16[20,32,128]{2,1,0:T(8,128)(2,1)S(1)} %get-tuple-element.29.going, f32[130,8,128]{2,1,0:T(8,128)S(1)} %get-tuple-element.30.dm_in, f32[128,8,128]{2,1,0:T(8,128)S(1)} %get-tuple-element.31.base, bf16[16,48,128]{2,1,0:T(8,128)(2,1)S(1)} %bitcast.26, ...), custom_call_target="tpu_custom_call" | custom-call | tf_op jit(solution)/shard_map/remap_return/pallas_call | solution.py:687
  64.8 1.7 %finish.1 = (f32[1024,128]{1,0:T(8,128)}, f32[1024,128]{1,0:T(8,128)}, f32[16,256]{1,0:T(8,128)}, f32[1,256]{1,0:T(1,128)}, f32[256,256]{1,0:T(8,128)}, /*index=...) custom-call(f32[1024,128]{1,0:T(8,128)S(1)} %get-tuple-element.33.adjoint_in, ...), custom_call_target="tpu_custom_call" | custom-call | tf_op jit(solution)/shard_map/finish/pallas_call | solution.py:718
  (2 shorter events, 0.0 us)
Async XLA Ops:
  0.6 14.9 %copy-start.5 = (f32[2,8]{1,0:T(2,128)S(1)}, f32[2,8]{1,0:T(2,128)}, u32[]{:S(2)}) copy-start(f32[2,8]{1,0:T(2,128)} %rate_in.1) | copy-start | bytes 196
  0.6 14.9 %copy-start.6 = (s32[1,1,1,64,4]{3,4,2,1,0:T(4,128)S(1)}, s32[1,1,1,64,4]{3,4,2,1,0:T(4,128)}, u32[]{:S(2)}) copy-start(s32[1,1,1,64,4]{3,4,2,1,0:T(4,128)} %param.28) | copy-start | bytes 3076
  0.7 14.9 %copy-start.10 = (f32[4]{0:T(128)S(1)}, f32[4]{0:T(128)}, u32[]{:S(2)}) copy-start(f32[4]{0:T(128)} %param.25) | copy-start | bytes 52
  0.7 14.9 %copy-start.7 = (bf16[256,4]{0,1:T(4,128)(2,1)S(1)}, bf16[256,4]{0,1:T(4,128)(2,1)}, u32[]{:S(2)}) copy-start(bf16[256,4]{0,1:T(4,128)(2,1)} %param.24) | copy-start | bytes 6148
  0.7 14.9 %copy-start.9 = (f32[256]{0:T(256)S(1)}, f32[256]{0:T(256)}, u32[]{:S(2)}) copy-start(f32[256]{0:T(256)} %param.23) | copy-start | bytes 3076
  0.7 14.9 %copy-start.1 = (bf16[256,256]{1,0:T(8,128)(2,1)S(1)}, bf16[256,256]{1,0:T(8,128)(2,1)}, u32[]{:S(2)}) copy-start(bf16[256,256]{1,0:T(8,128)(2,1)} %w_mid.1) | copy-start | bytes 393220
  0.7 14.9 %copy-start.8 = (f32[256]{0:T(256)S(1)}, f32[256]{0:T(256)}, u32[]{:S(2)}) copy-start(f32[256]{0:T(256)} %param.21) | copy-start | bytes 3076
  0.7 14.9 %copy-start.3 = (bf16[16,256]{1,0:T(8,128)(2,1)S(1)}, bf16[16,256]{1,0:T(8,128)(2,1)}, u32[]{:S(2)}) copy-start(bf16[16,256]{1,0:T(8,128)(2,1)} %w_in.1) | copy-start | bytes 24580
  0.7 14.9 %copy-start.4 = (f32[2,8,4]{1,2,0:T(4,128)S(1)}, f32[2,8,4]{1,2,0:T(4,128)}, u32[]{:S(2)}) copy-start(f32[2,8,4]{1,2,0:T(4,128)} %param.19) | copy-start | bytes 772
  0.7 14.9 %copy-start.2 = (s32[1,128,128]{2,1,0:T(8,128)S(1)}, s32[1,128,128]{2,1,0:T(8,128)}, u32[]{:S(2)}) copy-start(s32[1,128,128]{2,1,0:T(8,128)} %param.17) | copy-start | bytes 196612
  0.7 14.9 %copy-start = (f32[1,8,128,128]{3,2,1,0:T(8,128)S(1)}, f32[1,8,128,128]{3,2,1,0:T(8,128)}, u32[]{:S(2)}) copy-start(f32[1,8,128,128]{3,2,1,0:T(8,128)} %param.16) | copy-start | bytes 1572868
